TPU v7x, 128 devices: a whole 4x4x4 slice. The times are simulated.
128 devices in a mesh: seq: 32 (over y, z_lo, x), chan: 4 (over z_hi, core).
Axes of the slice: x: 4, y: 4, z: 4 (z_hi: 2, z_lo: 2; z = z_hi * 2 + z_lo), core: 2. Of those that a mesh axis runs over, the one named last changes fastest.
Arguments:
- base_ids: int32 [1, 32768], P(None, 'seq'), may hold values from 0 to 3
- embedding: bfloat16 [4, 1024], P(None, 'chan'), may hold values from -6 to 6
- gate_values: bfloat16 [1, 32768, 1024], P(None, 'seq', 'chan'), may hold values from -0.03125 to 0.03125
- filter_kernel: bfloat16 [32768, 1024], P('seq', 'chan'), may hold values from -0.03125 to 0.03125
- complement: int32 [1024], replicated, may hold values from 0 to 1023, as said below
- output_gradient: bfloat16 [1, 32768, 1024], P(None, 'seq', 'chan'), may hold values from -6 to 6
Outputs:
- gate_gradient: bfloat16 [1, 32768, 1024], P(None, 'seq', 'chan')
- filter_gradient: float32 [32768, 1024], P('seq', 'chan')
Inputs may be any that keep to these rules, and one draw needn't show every extreme that they name: complement[complement[c]] = c and complement[c] != c for every channel c: the channels come in complementary pairs.
All inputs are finite; a program needn't handle non-finite values.
Results may differ from a plain program's by a relative error of at most 0.012.
Values may be sent and summed in bfloat16 or wider, within the bound.
A program may use at most 64 MiB of HBM per device.

v0:
```python
import math

import jax
import jax.numpy as jnp
from jax import lax
from jax.sharding import PartitionSpec as P

TWO_PI = 2.0 * math.pi
HIGHEST = lax.Precision.HIGHEST


def angle_table(rows_count, cols_count, modulus):
    left_index = lax.broadcasted_iota(jnp.int32, (rows_count, cols_count), 0)
    right_index = lax.broadcasted_iota(jnp.int32, (rows_count, cols_count), 1)
    phase_index = left_index * right_index % modulus
    return TWO_PI * phase_index.astype(jnp.float32) / modulus


def build_tables(window, inner_width):
    outer_width = 2 * window // inner_width
    filled = window // inner_width
    outer_angle = angle_table(outer_width, filled, outer_width)
    outer_forward = jnp.concatenate([jnp.cos(outer_angle), -jnp.sin(outer_angle)], axis=0)
    forward_high = outer_forward.astype(jnp.bfloat16)
    forward_low = (outer_forward - forward_high.astype(jnp.float32)).astype(jnp.bfloat16)
    back_angle = angle_table(filled, outer_width, outer_width)
    back_cos = jnp.cos(back_angle) / outer_width
    back_sin = jnp.sin(back_angle) / outer_width
    outer_inverse = jnp.concatenate(
        [
            jnp.concatenate([back_cos, -back_sin], axis=1),
            jnp.concatenate([back_sin, back_cos], axis=1),
        ],
        axis=0,
    )
    twist_angle = angle_table(outer_width, inner_width, 2 * window)
    inner_angle = angle_table(inner_width, inner_width, inner_width)
    inner_cos = jnp.cos(inner_angle)
    inner_sin = jnp.sin(inner_angle)
    inner_table = jnp.concatenate(
        [
            jnp.concatenate([inner_cos, -inner_sin], axis=1),
            jnp.concatenate([inner_sin, inner_cos], axis=1),
        ],
        axis=0,
    )
    return (
        (forward_high, forward_low),
        outer_inverse,
        jnp.cos(twist_angle),
        jnp.sin(twist_angle),
        inner_table,
    )


def forward_spectra(signal, tables):
    forward_pair, outer_inverse, twist_cos, twist_sin, inner_table = tables
    forward_high, forward_low = forward_pair
    outer_width = twist_cos.shape[0]
    outer_mixed = jnp.einsum(
        "kh,zhn->zkn", forward_high, signal, preferred_element_type=jnp.float32
    )
    outer_mixed = outer_mixed + jnp.einsum(
        "kh,zhn->zkn", forward_low, signal, preferred_element_type=jnp.float32
    )
    real_part = outer_mixed[:, :outer_width]
    imag_part = outer_mixed[:, outer_width:]
    turned = jnp.concatenate(
        [
            real_part * twist_cos + imag_part * twist_sin,
            imag_part * twist_cos - real_part * twist_sin,
        ],
        axis=2,
    )
    return jnp.einsum("zkn,nm->zkm", turned, inner_table, precision=HIGHEST)


def inverse_fields(spectra, tables):
    forward_pair, outer_inverse, twist_cos, twist_sin, inner_table = tables
    inner_width = twist_cos.shape[1]
    unmixed = jnp.einsum("zkm,nm->zkn", spectra, inner_table, precision=HIGHEST) / inner_width
    real_part = unmixed[:, :, :inner_width]
    imag_part = unmixed[:, :, inner_width:]
    turned = jnp.concatenate(
        [
            real_part * twist_cos - imag_part * twist_sin,
            imag_part * twist_cos + real_part * twist_sin,
        ],
        axis=1,
    )
    return jnp.einsum("hk,zkn->zhn", outer_inverse, turned, precision=HIGHEST)


def parts_of(spectra):
    inner_width = spectra.shape[-1] // 2
    return (spectra[..., :inner_width], spectra[..., inner_width:])


def join_parts(real_part, imag_part):
    return jnp.concatenate([real_part, imag_part], axis=-1)


def to_senders(stacked, seq_count):
    sets_count, positions, channels = stacked.shape
    divided = stacked.reshape(sets_count, positions, seq_count, channels // seq_count)
    return divided.transpose(2, 3, 0, 1)


def from_senders(spread, inner_width):
    seq_count, share, sets_count, positions = spread.shape
    ordered = spread.transpose(1, 2, 0, 3)
    return ordered.reshape(share, sets_count, seq_count * positions // inner_width, inner_width)


def to_owners(outputs, seq_count, positions):
    share, sets_count = (outputs.shape[0], outputs.shape[1])
    return outputs.reshape(share, sets_count, seq_count, positions).transpose(2, 0, 1, 3)


def from_owners(returned):
    sets_count, positions = (returned.shape[2], returned.shape[3])
    return returned.reshape(-1, sets_count, positions).transpose(1, 2, 0)


def shards(base_ids, embedding, gate_values, filter_kernel, complement, output_gradient):
    seq_count = lax.axis_size("seq")
    batches, positions, channels = gate_values.shape
    window = positions * seq_count
    inner_width = math.gcd(positions, 256)
    filled = window // inner_width
    tables = build_tables(window, inner_width)
    letters = lax.broadcasted_iota(jnp.int32, (1, 1, embedding.shape[0]), 2)
    one_hot = (base_ids[:, :, None] == letters).astype(jnp.bfloat16)
    embedded = jnp.einsum("btv,vc->btc", one_hot, embedding, preferred_element_type=jnp.float32)
    conv_input = (gate_values.astype(jnp.float32) * embedded).astype(jnp.bfloat16)
    partner_index = lax.dynamic_slice_in_dim(
        complement, lax.axis_index("chan") * channels, channels
    )

    def partner_terms(signal):
        spectra = forward_spectra(signal, tables)
        half_sets = 1 + 2 * batches
        own_real, own_imag = parts_of(spectra[:half_sets])
        mate_real, mate_imag = parts_of(spectra[half_sets:])
        mix_real = own_real[0] + mate_real[0]
        mix_imag = mate_imag[0] - own_imag[0]
        grad_real = own_real[1 : 1 + batches]
        grad_imag = own_imag[1 : 1 + batches]
        input_real = own_real[1 + batches :]
        input_imag = own_imag[1 + batches :]
        mate_grad_real = mate_real[1 : 1 + batches]
        mate_grad_imag = mate_imag[1 : 1 + batches]
        mate_input_real = mate_real[1 + batches :]
        mate_input_imag = mate_imag[1 + batches :]
        step_real = grad_real * mix_real - grad_imag * mix_imag
        step_imag = grad_real * mix_imag + grad_imag * mix_real
        lag_real = jnp.sum(
            grad_real * input_real
            + grad_imag * input_imag
            + mate_input_real * mate_grad_real
            + mate_input_imag * mate_grad_imag,
            axis=0,
        )
        lag_imag = jnp.sum(
            grad_imag * input_real
            - grad_real * input_imag
            + mate_input_imag * mate_grad_real
            - mate_input_real * mate_grad_imag,
            axis=0,
        )
        combined = join_parts(
            jnp.concatenate([step_real, lag_real[None]], axis=0),
            jnp.concatenate([step_imag, lag_imag[None]], axis=0),
        )
        return inverse_fields(combined, tables)[:, :filled]

    whole_filter, whole_grad, whole_input = (
        lax.all_gather(filter_kernel, "chan", axis=1, tiled=True),
        lax.all_gather(output_gradient, "chan", axis=2, tiled=True),
        lax.all_gather(conv_input, "chan", axis=2, tiled=True),
    )
    stacked = jnp.concatenate(
        [
            filter_kernel[None],
            output_gradient,
            conv_input,
            jnp.take(whole_filter, partner_index, axis=1)[None],
            jnp.take(whole_grad, partner_index, axis=2),
            jnp.take(whole_input, partner_index, axis=2),
        ],
        axis=0,
    )
    spread = lax.all_to_all(
        to_senders(stacked, seq_count), "seq", split_axis=0, concat_axis=0, tiled=True
    )
    outputs = lax.map(partner_terms, from_senders(spread, inner_width))
    returned = lax.all_to_all(
        to_owners(outputs, seq_count, positions), "seq", split_axis=0, concat_axis=1, tiled=True
    )
    result = from_owners(returned)
    filter_gradient = result[batches]
    gate_gradient = (result[:batches] * embedded).astype(jnp.bfloat16)
    return (gate_gradient, filter_gradient)


def solution(mesh):
    in_specs = (
        P(None, "seq"),
        P(None, "chan"),
        P(None, "seq", "chan"),
        P("seq", "chan"),
        P(),
        P(None, "seq", "chan"),
    )
    out_specs = (P(None, "seq", "chan"), P("seq", "chan"))
    return jax.shard_map(shards, mesh=mesh, in_specs=in_specs, out_specs=out_specs, check_vma=False)
```

profile of v0, /device:TPU:1, one launch (start us, length us, event | category | flops | bytes accessed | tf_op | source)
XLA Modules:
  0.0 335.9 jit_solution(1141070171212983378)
XLA Ops:
  7.2 2.0 copy.39
  13.8 1.8 bitcast_dynamic-update-slice_fusion
  17.2 23.5 %all-gather.6.cloned.1.call-done = bf16[1,1024,1024]{1,2,0:T(8,128)(2,1)} async-done(((bf16[1,1024,256]{1,2,0:T(8,128)(2,1)}), bf16[1,1024,1024]{1,2,0:T(8,128)(2,1)}) %all-gather.6.cloned.1.call-update) | async-done | bytes 2097168 | tf_op jit(solution)/shard_map/all_gather | solution.py:179
  40.7 3.4 %gather_fusion.1 = bf16[256,1024]{1,0:T(8,128)(2,1)S(1)} fusion(bf16[1024,1024]{0,1:T(8,128)(2,1)} %bitcast.103, s32[1024]{0:T(1024)S(1)} %pad_clamp_fusion), kind=kCustom, calls=%fused_computation.clone | custom fusion | bytes 1049600 | tf_op jit(solution)/shard_map/jit(_take)/gather | solution.py:188
  44.1 24.2 %all-gather.8.cloned.1.call-done = bf16[1,1024,1024]{1,2,0:T(8,128)(2,1)} async-done(((bf16[1,1024,256]{1,2,0:T(8,128)(2,1)}), bf16[1,1024,1024]{1,2,0:T(8,128)(2,1)}) %all-gather.8.cloned.1.call-update) | async-done | bytes 2097168 | tf_op jit(solution)/shard_map/all_gather | solution.py:180
  68.4 3.4 %gather_fusion.2 = bf16[256,1024]{1,0:T(8,128)(2,1)S(1)} fusion(bf16[1024,1024]{0,1:T(8,128)(2,1)} %bitcast.104, s32[1024]{0:T(1024)S(1)} %pad_clamp_fusion), kind=kCustom, calls=%fused_computation.1.clone | custom fusion | bytes 1049600 | tf_op jit(solution)/shard_map/jit(_take)/gather | solution.py:189
  71.8 24.3 %all-gather.4.cloned.1.call-done = bf16[1024,1024]{0,1:T(8,128)(2,1)} async-done(((bf16[1024,256]{0,1:T(8,128)(2,1)}), bf16[1024,1024]{0,1:T(8,128)(2,1)}) %all-gather.4.cloned.1.call-update) | async-done | bytes 2097168 | tf_op jit(solution)/shard_map/all_gather | solution.py:178
  96.1 3.4 %gather_fusion = bf16[256,1024]{1,0:T(8,128)(2,1)S(1)} fusion(bf16[1024,1024]{0,1:T(8,128)(2,1)} %all-gather.4.cloned.1.call-done, s32[1024]{0:T(1024)S(1)} %pad_clamp_fusion), kind=kCustom, calls=%fused_computation.2 | custom fusion | bytes 1049600 | tf_op jit(solution)/shard_map/jit(_take)/gather | solution.py:187
  102.3 4.0 %copy.43 = bf16[32,8,6,1024]{3,1,2,0:T(8,128)(2,1)} copy(bf16[32,8,6,1024]{3,1,0,2:T(8,128)(2,1)} %bitcast.15) | data formatting | bytes 6291456 | tf_op jit(solution)/shard_map/transpose | solution.py:106
  106.3 7.2 %all-to-all-start = ((bf16[32,8,6,1024]{3,1,2,0:T(8,128)(2,1)}), bf16[32,8,6,1024]{3,1,2,0:T(8,128)(2,1)}, u32[]{:S(2)}, u32[]{:S(2)}) async-start(bf16[32,8,6,1024]{3,1,2,0:T(8,128)(2,1)} %copy.43), calls=%async_computation | async-start | bytes 6291456 | tf_op jit(solution)/shard_map/all_to_all | solution.py:193
  118.0 34.6 %all-to-all-done = bf16[32,8,6,1024]{3,1,2,0:T(8,128)(2,1)} async-done(((bf16[32,8,6,1024]{3,1,2,0:T(8,128)(2,1)}), bf16[32,8,6,1024]{3,1,2,0:T(8,128)(2,1)}, u32[]{:S(2)}, u32[]{:S(2)}) %all-to-all-start) | async-done | bytes 3145760 | tf_op jit(solution)/shard_map/all_to_all | solution.py:193
  152.6 5.3 %copy.44 = bf16[8,6,32,1024]{3,2,1,0:T(8,128)(2,1)} copy(bf16[8,6,32,1024]{3,0,1,2:T(8,128)(2,1)} %bitcast.16) | data formatting | bytes 6291456 | tf_op jit(solution)/shard_map/transpose | solution.py:111
  157.9 5.9 %reshape.112 = bf16[8,6,128,256]{3,2,1,0:T(8,128)(2,1)} reshape(bf16[8,6,32,1024]{3,2,1,0:T(8,128)(2,1)} %copy.44) | data formatting | bytes 6291456 | tf_op jit(solution)/shard_map/reshape | solution.py:112
  163.8 124.2 %while.12 = (s32[]{:T(128)}, f32[8,2,128,256]{3,2,1,0:T(8,128)}, bf16[8,6,128,256]{3,2,1,0:T(8,128)(2,1)}, bf16[512,128]{1,0:T(8,128)(2,1)S(1)}, bf16[512,128]{1...) while((s32[]{:T(128)}, f32[8,2,128,256]{3,2,1,0:T(8,128)}, ...), condition=%wide.region_1.3_spmd.clone.clone, body=%wide.region_0.2_spmd.clone.clone.sunk | while | flops 7658930176 | bytes 42993236 | solution.py:196
  165.4 1.6 add_bitcast_fusion.2
  168.5 5.4 %fusion.98 = f32[6,256,512]{2,1,0:T(8,128)S(1)} fusion(f32[6,256,256]{1,2,0:T(8,128)S(1)} %get-tuple-element.227, f32[6,256,256]{1,2,0:T(8,128)S(1)} %get-tuple-element.228, f32[512,512]{1,0:T(8,128)S(1)} %get-tuple-element.256), kind=kOutput, calls=%fused_computation.5.clone.1 | convolution fusion | flops 4832624640 | bytes 7340032 | tf_op jit(solution)/shard_map/while/body/eval_jaxpr/zkn,nm->zkm/dot_general | solution.py:75
  174.3 1.9 convolution_multiply_fusion.2
  176.6 1.9 convolution_bitcast_fusion.3
  180.9 1.6 add_bitcast_fusion.2
  184.0 5.4 %fusion.98 = f32[6,256,512]{2,1,0:T(8,128)S(1)} fusion(f32[6,256,256]{1,2,0:T(8,128)S(1)} %get-tuple-element.227, f32[6,256,256]{1,2,0:T(8,128)S(1)} %get-tuple-element.228, f32[512,512]{1,0:T(8,128)S(1)} %get-tuple-element.256), kind=kOutput, calls=%fused_computation.5.clone.1 | convolution fusion | flops 4832624640 | bytes 7340032 | tf_op jit(solution)/shard_map/while/body/eval_jaxpr/zkn,nm->zkm/dot_general | solution.py:75
  189.8 1.9 convolution_multiply_fusion.2
  192.1 1.9 convolution_bitcast_fusion.3
  196.4 1.6 add_bitcast_fusion.2
  199.5 5.4 %fusion.98 = f32[6,256,512]{2,1,0:T(8,128)S(1)} fusion(f32[6,256,256]{1,2,0:T(8,128)S(1)} %get-tuple-element.227, f32[6,256,256]{1,2,0:T(8,128)S(1)} %get-tuple-element.228, f32[512,512]{1,0:T(8,128)S(1)} %get-tuple-element.256), kind=kOutput, calls=%fused_computation.5.clone.1 | convolution fusion | flops 4832624640 | bytes 7340032 | tf_op jit(solution)/shard_map/while/body/eval_jaxpr/zkn,nm->zkm/dot_general | solution.py:75
  205.3 1.9 convolution_multiply_fusion.2
  207.6 1.9 convolution_bitcast_fusion.3
  212.0 1.6 add_bitcast_fusion.2
  215.0 5.4 %fusion.98 = f32[6,256,512]{2,1,0:T(8,128)S(1)} fusion(f32[6,256,256]{1,2,0:T(8,128)S(1)} %get-tuple-element.227, f32[6,256,256]{1,2,0:T(8,128)S(1)} %get-tuple-element.228, f32[512,512]{1,0:T(8,128)S(1)} %get-tuple-element.256), kind=kOutput, calls=%fused_computation.5.clone.1 | convolution fusion | flops 4832624640 | bytes 7340032 | tf_op jit(solution)/shard_map/while/body/eval_jaxpr/zkn,nm->zkm/dot_general | solution.py:75
  220.9 1.9 convolution_multiply_fusion.2
  223.1 1.9 convolution_bitcast_fusion.3
  227.5 1.6 add_bitcast_fusion.2
  230.5 5.4 %fusion.98 = f32[6,256,512]{2,1,0:T(8,128)S(1)} fusion(f32[6,256,256]{1,2,0:T(8,128)S(1)} %get-tuple-element.227, f32[6,256,256]{1,2,0:T(8,128)S(1)} %get-tuple-element.228, f32[512,512]{1,0:T(8,128)S(1)} %get-tuple-element.256), kind=kOutput, calls=%fused_computation.5.clone.1 | convolution fusion | flops 4832624640 | bytes 7340032 | tf_op jit(solution)/shard_map/while/body/eval_jaxpr/zkn,nm->zkm/dot_general | solution.py:75
  236.4 1.9 convolution_multiply_fusion.2
  238.7 1.9 convolution_bitcast_fusion.3
  243.0 1.6 add_bitcast_fusion.2
  246.1 5.4 %fusion.98 = f32[6,256,512]{2,1,0:T(8,128)S(1)} fusion(f32[6,256,256]{1,2,0:T(8,128)S(1)} %get-tuple-element.227, f32[6,256,256]{1,2,0:T(8,128)S(1)} %get-tuple-element.228, f32[512,512]{1,0:T(8,128)S(1)} %get-tuple-element.256), kind=kOutput, calls=%fused_computation.5.clone.1 | convolution fusion | flops 4832624640 | bytes 7340032 | tf_op jit(solution)/shard_map/while/body/eval_jaxpr/zkn,nm->zkm/dot_general | solution.py:75
  251.9 1.9 convolution_multiply_fusion.2
  254.2 1.9 convolution_bitcast_fusion.3
  258.5 1.6 add_bitcast_fusion.2
  261.6 5.4 %fusion.98 = f32[6,256,512]{2,1,0:T(8,128)S(1)} fusion(f32[6,256,256]{1,2,0:T(8,128)S(1)} %get-tuple-element.227, f32[6,256,256]{1,2,0:T(8,128)S(1)} %get-tuple-element.228, f32[512,512]{1,0:T(8,128)S(1)} %get-tuple-element.256), kind=kOutput, calls=%fused_computation.5.clone.1 | convolution fusion | flops 4832624640 | bytes 7340032 | tf_op jit(solution)/shard_map/while/body/eval_jaxpr/zkn,nm->zkm/dot_general | solution.py:75
  267.4 1.9 convolution_multiply_fusion.2
  269.7 1.9 convolution_bitcast_fusion.3
  274.1 1.6 add_bitcast_fusion.2
  277.2 5.4 %fusion.98 = f32[6,256,512]{2,1,0:T(8,128)S(1)} fusion(f32[6,256,256]{1,2,0:T(8,128)S(1)} %get-tuple-element.227, f32[6,256,256]{1,2,0:T(8,128)S(1)} %get-tuple-element.228, f32[512,512]{1,0:T(8,128)S(1)} %get-tuple-element.256), kind=kOutput, calls=%fused_computation.5.clone.1 | convolution fusion | flops 4832624640 | bytes 7340032 | tf_op jit(solution)/shard_map/while/body/eval_jaxpr/zkn,nm->zkm/dot_general | solution.py:75
  283.0 1.9 convolution_multiply_fusion.2
  285.3 1.9 convolution_bitcast_fusion.3
  288.0 1.8 reshape.113
  291.5 34.0 %all_to_all.14 = f32[32,8,2,1024]{3,2,1,0:T(2,128)S(1)} all-to-all(f32[32,8,2,1024]{3,2,1,0:T(2,128)S(1)} %copy.47), channel_id=1, replica_groups=mesh['seq'=32,'chan'=4] {'seq'}, dimensions={0} | all-to-all | bytes 4194304 | tf_op jit(solution)/shard_map/all_to_all | solution.py:197
  (129 shorter events, 56.3 us)
Async XLA Ops:
  7.2 6.6 %copy-start = (bf16[4,256]{1,0:T(4,128)(2,1)S(1)}, bf16[4,256]{1,0:T(4,128)(2,1)}, u32[]{:S(2)}) copy-start(bf16[4,256]{1,0:T(4,128)(2,1)} %param.11) | copy-start | bytes 6148
  7.2 6.6 %copy-start.4 = (s32[1,1024]{1,0:T(1,128)S(1)}, s32[1,1024]{1,0:T(1,128)}, u32[]{:S(2)}) copy-start(s32[1,1024]{1,0:T(1,128)} %param.10) | copy-start | bytes 12292
  7.2 33.5 %all-gather.6.cloned.1.call-start = ((), (), s32[]{:S(2)}) async-start(), calls=%async_computation.3 | async-start | bytes 2621440 | tf_op jit(solution)/shard_map/all_gather | solution.py:179
  9.3 3.7 %copy-start.2 = (bf16[1,1024,256]{1,2,0:T(8,128)(2,1)S(1)}, bf16[1,1024,256]{1,2,0:T(8,128)(2,1)}, u32[]{:S(2)}) copy-start(bf16[1,1024,256]{1,2,0:T(8,128)(2,1)} %copy.39) | copy-start | bytes 1572868
  9.3 59.1 %all-gather.8.cloned.1.call-start = ((), (), s32[]{:S(2)}) async-start(), calls=%async_computation.4 | async-start | bytes 2621440 | tf_op jit(solution)/shard_map/all_gather | solution.py:180
  10.7 5.0 %copy-start.1 = (bf16[1024,256]{0,1:T(8,128)(2,1)}, bf16[1024,256]{0,1:T(8,128)(2,1)S(1)}, u32[]{:S(2)}) copy-start(bf16[1024,256]{0,1:T(8,128)(2,1)S(1)} %copy.38) | copy-start | bytes 1572868
  15.6 80.4 %all-gather.4.cloned.1.call-start = ((), (), s32[]{:S(2)}) async-start(), calls=%async_computation.2 | async-start | bytes 2621440 | tf_op jit(solution)/shard_map/all_gather | solution.py:178
  106.3 46.2 %all-to-all-start = ((bf16[32,8,6,1024]{3,1,2,0:T(8,128)(2,1)}), bf16[32,8,6,1024]{3,1,2,0:T(8,128)(2,1)}, u32[]{:S(2)}, u32[]{:S(2)}) async-start(bf16[32,8,6,1024]{3,1,2,0:T(8,128)(2,1)} %copy.43), calls=%async_computation | async-start | bytes 6291456 | tf_op jit(solution)/shard_map/all_to_all | solution.py:193
  325.5 1.2 copy-start.3
Sparse Core Ops, SparseCore 0:
  10.3 30.3 all-gather.5
  42.4 25.9 all-gather.7
  70.0 25.9 all-gather.3
where the time goes:
time: 339 us; the launch traced here: 336 us
  waiting for transfers between devices  107 us (32%)
  matrix products  101 us (30%)
  local copies, waits for them, and re-layouts  48.1 us (14%)
  blocking collectives  34 us (10%)
  other arithmetic  24 us (7%)
  between operations  13.9 us (4%)
  starting transfers between devices  7.32 us (2%)
    dot_general x8, matrix products, forward_spectra(): return jnp.einsum('zkn,nm->zkm', turned, inner_table, precision=HIGHEST)  43.2 us
    all_to_all x1, waiting for transfers between devices, shards(): lax.all_to_all(to_senders(stacked, seq_count), 'seq', split_axis=0, conca...  34.6 us
    all_to_all x1, blocking collectives, shards(): lax.all_to_all(to_owners(outputs, seq_count, positions), 'seq', split_axi...  34 us
    all_gather x1, waiting for transfers between devices, shards(): lax.all_gather(filter_kernel, 'chan', axis=1, tiled=True)  24.3 us
    all_gather x1, waiting for transfers between devices, shards(): lax.all_gather(conv_input, 'chan', axis=2, tiled=True)  24.2 us
    all_gather x1, waiting for transfers between devices, shards(): lax.all_gather(output_gradient, 'chan', axis=2, tiled=True)  23.5 us
    dot_general x8, matrix products, inverse_fields(): jnp.einsum('zkm,nm->zkn', spectra, inner_table, precision=HIGHEST)  14.9 us
    dot_general x8, matrix products, inverse_fields(): return jnp.einsum('hk,zkn->zhn', outer_inverse, turned, precision=HIGHEST)  14.8 us
  transfers between devices with their start and end apart: 4, of which 4 were waited for; matrix products, arithmetic and copies ran while one was open for 5% of the time, Pallas kernels for 0%

commit v1 on v0

v1 whole, which is shorter than its diff:
```python
import functools
import itertools
import math

import jax
import jax.numpy as jnp
import numpy as np
from jax import lax
from jax.experimental import pallas as pl
from jax.experimental.pallas import tpu as pltpu
from jax.sharding import PartitionSpec as P

MESH = pl.DeviceIdType.MESH
F32 = jnp.float32
BF16 = jnp.bfloat16
SHARDS = 4
SEQ_DEVICES = 32
DEVICES = SHARDS * SEQ_DEVICES
LANES = 128
ROWS = 8
LENGTH = 32768
SHARE = 2 * SHARDS
INNER = 128
OUTER = LENGTH // INNER
HALF = 2 * ROWS
CHANNELS = 256
ALL_CHANNELS = SHARDS * CHANNELS


def two_factors():
    edges = [(a, b) for a in range(SHARDS) for b in range(a, SHARDS)]
    found = []
    for chosen in itertools.combinations_with_replacement(edges, SHARDS):
        degrees = [sum(edge.count(shard) for edge in chosen) for shard in range(SHARDS)]
        if degrees == [2] * SHARDS:
            found.append(chosen)
    return found


def slots_of(chosen):
    used = [0] * SHARDS
    ends = []
    partner = [0] * SHARE
    for a, b in chosen:
        first = used[a]
        used[a] += 1
        second = used[b]
        used[b] += 1
        ends.append((first, second))
        partner[2 * a + first] = 2 * b + second
        partner[2 * b + second] = 2 * a + first
    return ends, partner


FACTORS = [(chosen, *slots_of(chosen)) for chosen in two_factors()]


def split(table):
    high = table.astype(np.float32).astype(jnp.bfloat16)
    low = (table.astype(np.float32) - high.astype(np.float32)).astype(jnp.bfloat16)
    return np.stack([high, low])


def transform_tables():
    window = 2 * LENGTH
    k = np.arange(OUTER)[:, None] + 0.5
    outer_angle = 2 * np.pi * k * np.arange(OUTER)[None] / (2 * OUTER)
    outer = np.concatenate([np.cos(outer_angle), -np.sin(outer_angle)], axis=0)
    m = np.arange(INNER)
    inner_angle = 2 * np.pi * ((m[:, None] * m[None]) % INNER) / INNER
    c, s = np.cos(inner_angle), np.sin(inner_angle)
    inner = np.block([[c, -s], [s, c]])
    twist = 2 * np.pi * k * m[None] / window
    twists = np.stack([np.cos(twist), np.sin(twist)]).astype(np.float32)
    return split(outer), split(outer.T * (2.0 / window)), split(inner), split(inner.T), twists


def device_at(step, seq, chan):
    sy, sz, sx = lax.div(seq, 8), lax.rem(lax.div(seq, 4), 2), lax.rem(seq, 4)
    z = lax.div(chan, 2) * 2 + sz
    core = lax.rem(chan, 2)
    x2 = lax.rem(sx + lax.rem(step, 4), 4)
    y2 = lax.rem(sy + lax.rem(lax.div(step, 4), 4), 4)
    z2 = lax.rem(z + lax.rem(lax.div(step, 16), 4), 4)
    core2 = lax.rem(core + lax.div(step, 64), 2)
    return y2 * 8 + lax.rem(z2, 2) * 4 + x2, lax.div(z2, 2) * 2 + core2


def route(comp_ref, seq, chan, perm_ref):
    comp = comp_ref[...]
    every = lax.broadcasted_iota(jnp.int32, (1, ALL_CHANNELS), 1)
    low, high = jnp.minimum(comp, every), jnp.maximum(comp, every)
    kind = lax.div(low, CHANNELS) * SHARDS + lax.div(high, CHANNELS)
    kind = jnp.where(every < comp, kind, -1)
    kinds = lax.broadcasted_iota(jnp.int32, (16, ALL_CHANNELS), 0)
    hot = jnp.where(kinds == kind, 1.0, 0.0).astype(BF16)
    start = pl.multiple_of(chan * CHANNELS, CHANNELS)
    own_comp = comp_ref[:, pl.ds(start, CHANNELS)]
    own = lax.broadcasted_iota(jnp.int32, (1, CHANNELS), 1) + start
    own_low, own_high = jnp.minimum(own_comp, own), jnp.maximum(own_comp, own)
    own_first = own < own_comp
    own_kind = lax.div(own_low, CHANNELS) * SHARDS + lax.div(own_high, CHANNELS)
    before = lax.broadcasted_iota(jnp.int32, (ALL_CHANNELS, CHANNELS), 0) < own_low
    before = jnp.where(before, 1.0, 0.0).astype(BF16)
    ranks = jnp.dot(hot, before, preferred_element_type=F32)
    own_kinds = lax.broadcasted_iota(jnp.int32, (16, CHANNELS), 0) == own_kind
    rank = jnp.sum(jnp.where(own_kinds, ranks, 0.0), axis=0, keepdims=True)
    totals = jnp.dot(hot, jnp.ones((ALL_CHANNELS, CHANNELS), BF16), preferred_element_type=F32)
    rank = rank.astype(jnp.int32)
    totals = totals.astype(jnp.int32)
    left = {edge: totals[edge[0] * SHARDS + edge[1]][None] for edge in {e for f in FACTORS for e in f[0]}}
    taken = {edge: jnp.zeros((1, CHANNELS), jnp.int32) for edge in left}
    begin = jnp.zeros((1, CHANNELS), jnp.int32)
    me = chan * SEQ_DEVICES + seq
    place = jnp.zeros((1, CHANNELS), jnp.int32)
    code = jnp.zeros((1, CHANNELS), jnp.int32)
    for chosen, ends, partner in FACTORS:
        count = None
        for edge in set(chosen):
            possible = left[edge] if chosen.count(edge) == 1 else lax.shift_right_logical(left[edge], 1)
            count = possible if count is None else jnp.minimum(count, possible)
        for edge in sorted(set(chosen)):
            times = chosen.count(edge)
            first, second = ends[chosen.index(edge)]
            offset = rank - taken[edge]
            size = count * times
            here = (own_kind == edge[0] * SHARDS + edge[1]) & (offset >= 0) & (offset < size)
            if times == 2:
                spot = 2 * begin + offset
            else:
                spot = 2 * (begin + offset) + jnp.where(own_first, first, second)
            place = jnp.where(here, spot, place)
            left[edge] = left[edge] - size
            taken[edge] = taken[edge] + size
        mine = (begin <= me) & (me < begin + count)
        code = jnp.where(mine, sum(p << (3 * i) for i, p in enumerate(partner)), code)
        begin = begin + count
    slots = lax.broadcasted_iota(jnp.int32, (CHANNELS, CHANNELS), 0)
    perm_ref[...] = jnp.where(slots == place, 1.0, 0.0).astype(BF16)
    return jnp.max(code)


def kernel(
    ids_hbm, emb_hbm, gate_hbm, filt_hbm, comp_hbm, grad_hbm,
    outer_hbm, outer_back_hbm, inner_hbm, inner_back_hbm, twist_hbm,
    gate_out, filt_out,
    ids, emb, gate, filt, comp, grad,
    outer, outer_back, inner, inner_back, twist,
    perm, strided, letters, embedded, spectra,
    send_k, send_g, send_u, recv_k, recv_g, recv_u,
    send_du, send_dk, recv_du, recv_dk, gate_vmem, filt_vmem,
    load_sem, store_sem, local_sem, send_sem, recv_sem,
):
    seq, chan = lax.axis_index("seq"), lax.axis_index("chan")
    me = chan * SEQ_DEVICES + seq
    loads = {}
    sources = [
        (comp_hbm, comp), (ids_hbm, ids), (emb_hbm, emb), (filt_hbm, filt), (grad_hbm, grad), (gate_hbm, gate),
        (outer_hbm, outer), (twist_hbm, twist), (inner_hbm, inner), (inner_back_hbm, inner_back),
        (outer_back_hbm, outer_back),
    ]
    for index, (source, target) in enumerate(sources):
        loads[index] = pltpu.make_async_copy(source, target, load_sem.at[index])
        loads[index].start()

    barrier = pltpu.get_barrier_semaphore()

    def greet(step, carry):
        pl.semaphore_signal(barrier, inc=1, device_id=device_at(step, seq, chan), device_id_type=MESH)
        return carry

    lax.fori_loop(1, DEVICES, greet, 0)

    loads[0].wait()
    code = route(comp, seq, chan, perm)

    def lay_out(source_of, target):
        for a in range(ROWS):
            strided[pl.ds(a, CHANNELS, stride=ROWS), :] = source_of(a)
        target[...] = strided[...].reshape(DEVICES, HALF, LANES).astype(BF16)

    def turned(ref):
        def part(a):
            block = ref[pl.ds(a * LANES, LANES), :]
            return lax.dot_general(perm[...], block, (((1,), (1,)), ((), ())), preferred_element_type=F32)
        return part

    def post(source, target, index):
        pltpu.make_async_copy(source.at[me], target.at[me], local_sem.at[index]).start()

        def one(step, carry):
            seq2, chan2 = device_at(lax.rem(step * 37, DEVICES), seq, chan)
            pltpu.make_async_remote_copy(
                source.at[chan2 * SEQ_DEVICES + seq2], target.at[me], send_sem.at[index], recv_sem.at[index],
                device_id=(seq2, chan2), device_id_type=MESH,
            ).start()
            return carry

        lax.fori_loop(1, DEVICES, one, 0)

    def arrived(source, target, index):
        pltpu.make_async_copy(source.at[me], target.at[me], local_sem.at[index]).wait()
        rest = pl.ds(0, DEVICES - 1)
        pltpu.make_async_copy(target.at[rest], target.at[rest], recv_sem.at[index]).wait()

    def left_here(source, index):
        rest = pl.ds(0, DEVICES - 1)
        pltpu.make_async_copy(source.at[rest], source.at[rest], send_sem.at[index]).wait()

    loads[3].wait()
    lay_out(turned(filt), send_k)
    pl.semaphore_wait(barrier, DEVICES - 1)
    post(send_k, recv_k, 0)

    loads[4].wait()
    lay_out(turned(grad), send_g)
    post(send_g, recv_g, 1)

    loads[1].wait()
    loads[2].wait()
    names = lax.broadcasted_iota(jnp.int32, (4, ALL_CHANNELS), 0)
    letters[...] = jnp.where(names == ids[...], 1.0, 0.0).astype(BF16)
    own_emb = lax.dot_general(perm[...], emb[...], (((1,), (1,)), ((), ())), preferred_element_type=F32).astype(BF16)
    for a in range(ROWS):
        embedded[a] = jnp.dot(own_emb, letters[:, a * LANES : (a + 1) * LANES], preferred_element_type=F32)
    loads[5].wait()
    turn_gate = turned(gate)
    lay_out(lambda a: turn_gate(a) * embedded[a], send_u)
    post(send_u, recv_u, 2)

    for index in range(6, 11):
        loads[index].wait()

    def times(matrices, right):
        return jnp.dot(matrices[0], right, preferred_element_type=F32) + jnp.dot(
            matrices[1], right, preferred_element_type=F32
        )

    def times_right(left, matrices):
        return jnp.dot(left, matrices[0], preferred_element_type=F32) + jnp.dot(
            left, matrices[1], preferred_element_type=F32
        )

    def forward(received, shard):
        block = received[pl.ds(shard * SEQ_DEVICES, SEQ_DEVICES)].astype(F32)
        block = block.reshape(SEQ_DEVICES, 2, ROWS, LANES)
        fields = [block[:, slot].reshape(OUTER, INNER) for slot in range(2)]
        mixed = times(outer, jnp.concatenate(fields, axis=1).astype(BF16))
        cos, sin = twist[0], twist[1]
        spread = []
        for slot in range(2):
            real = mixed[:OUTER, slot * INNER : (slot + 1) * INNER]
            imag = mixed[OUTER:, slot * INNER : (slot + 1) * INNER]
            spread.append(jnp.concatenate([real * cos + imag * sin, imag * cos - real * sin], axis=1))
        return times_right(jnp.concatenate(spread, axis=0).astype(BF16), inner)

    def backward(parts):
        rows = [jnp.concatenate([real, imag], axis=1) for real, imag in parts]
        mixed = times_right(jnp.concatenate(rows, axis=0).astype(BF16), inner_back)
        cos, sin = twist[0], twist[1]
        spread = []
        for slot in range(2):
            real = mixed[slot * OUTER : (slot + 1) * OUTER, :INNER]
            imag = mixed[slot * OUTER : (slot + 1) * OUTER, INNER:]
            spread.append(jnp.concatenate([real * cos - imag * sin, imag * cos + real * sin], axis=0))
        fields = times(outer_back, jnp.concatenate(spread, axis=1).astype(BF16))
        halves = [
            fields[:, slot * INNER : (slot + 1) * INNER].reshape(SEQ_DEVICES, 1, ROWS, LANES) for slot in range(2)
        ]
        return jnp.concatenate(halves, axis=1).reshape(SEQ_DEVICES, HALF, LANES).astype(BF16)

    def spectrum(kind, channel):
        both = spectra[kind * SHARE + channel]
        return both[:, :INNER], both[:, INNER:]

    def partner_of(channel):
        return lax.rem(lax.shift_right_logical(code, 3 * channel), SHARE)

    def all_forward(received, kind, finish):
        def body(shard, carry):
            both = forward(received, shard)
            for slot in range(2):
                channel = 2 * shard + slot
                spectra[kind * SHARE + channel] = finish(both[slot * OUTER : (slot + 1) * OUTER], channel)
            return carry

        lax.fori_loop(0, SHARDS, body, 0)

    def all_backward(combine, source, target, index):
        pltpu_local = pltpu.make_async_copy(source.at[me], target.at[me], local_sem.at[index])

        def body(turn, carry):
            shard = lax.rem(chan + turn, SHARDS)
            base = shard * SEQ_DEVICES
            source[pl.ds(base, SEQ_DEVICES)] = backward([combine(2 * shard + slot) for slot in range(2)])

            @pl.when(turn == 0)
            def _():
                pltpu_local.start()

            def one(step, inner_carry):
                seq2 = lax.rem(seq + step, SEQ_DEVICES)
                pltpu.make_async_remote_copy(
                    source.at[base + seq2], target.at[me], send_sem.at[index], recv_sem.at[index],
                    device_id=(seq2, shard), device_id_type=MESH,
                ).start()
                return inner_carry

            lax.fori_loop(jnp.where(turn == 0, 1, 0), SEQ_DEVICES, one, 0)
            return carry

        lax.fori_loop(0, SHARDS, body, 0)

    arrived(send_k, recv_k, 0)
    all_forward(recv_k, 0, lambda both, channel: both)
    arrived(send_g, recv_g, 1)
    all_forward(recv_g, 1, lambda both, channel: both)

    def input_spectrum(channel):
        k_real, k_imag = spectrum(0, channel)
        p_real, p_imag = spectrum(0, partner_of(channel))
        g_real, g_imag = spectrum(1, channel)
        real, imag = k_real + p_real, p_imag - k_imag
        return g_real * real - g_imag * imag, g_real * imag + g_imag * real

    all_backward(input_spectrum, send_du, recv_du, 3)

    def product(both, channel):
        g_real, g_imag = spectrum(1, channel)
        u_real, u_imag = both[:, :INNER], both[:, INNER:]
        return jnp.concatenate([g_real * u_real + g_imag * u_imag, g_imag * u_real - g_real * u_imag], axis=1)

    arrived(send_u, recv_u, 2)
    all_forward(recv_u, 2, product)

    def filter_spectrum(channel):
        real, imag = spectrum(2, channel)
        p_real, p_imag = spectrum(2, partner_of(channel))
        return real + p_real, imag - p_imag

    all_backward(filter_spectrum, send_dk, recv_dk, 4)

    def give_back(received, scale, target):
        strided[...] = received[...].astype(F32).reshape(DEVICES * HALF, LANES)
        for a in range(ROWS):
            part = scale(strided[pl.ds(a, CHANNELS, stride=ROWS), :], a).astype(BF16)
            block = lax.dot_general(part, perm[...], (((0,), (0,)), ((), ())), preferred_element_type=F32)
            target[pl.ds(a * LANES, LANES), :] = block.astype(target.dtype)

    arrived(send_du, recv_du, 3)
    give_back(recv_du, lambda part, a: part * embedded[a], gate_vmem)
    gate_store = pltpu.make_async_copy(gate_vmem, gate_out, store_sem.at[0])
    gate_store.start()
    arrived(send_dk, recv_dk, 4)
    give_back(recv_dk, lambda part, a: part, filt_vmem)
    filt_store = pltpu.make_async_copy(filt_vmem, filt_out, store_sem.at[1])
    filt_store.start()
    for index, source in enumerate([send_k, send_g, send_u, send_du, send_dk]):
        left_here(source, index)
    gate_store.wait()
    filt_store.wait()


def shards(base_ids, embedding, gate_values, filter_kernel, complement, output_gradient):
    positions, channels = filter_kernel.shape
    tables = transform_tables()
    blocks = pltpu.VMEM((DEVICES, HALF, LANES), BF16)
    gate_gradient, filter_gradient = pl.pallas_call(
        kernel,
        out_shape=[
            jax.ShapeDtypeStruct((positions, channels), BF16),
            jax.ShapeDtypeStruct((positions, channels), F32),
        ],
        in_specs=[pl.BlockSpec(memory_space=pl.ANY)] * 11,
        out_specs=[pl.BlockSpec(memory_space=pl.ANY)] * 2,
        scratch_shapes=[
            pltpu.VMEM((1, positions), jnp.int32),
            pltpu.VMEM(embedding.shape, BF16),
            pltpu.VMEM((positions, channels), BF16),
            pltpu.VMEM((positions, channels), BF16),
            pltpu.VMEM((1, ALL_CHANNELS), jnp.int32),
            pltpu.VMEM((positions, channels), BF16),
            *[pltpu.VMEM(table.shape, table.dtype) for table in tables],
            pltpu.VMEM((channels, channels), BF16),
            pltpu.VMEM((DEVICES * HALF, LANES), F32),
            pltpu.VMEM((4, positions), BF16),
            pltpu.VMEM((ROWS, channels, LANES), F32),
            pltpu.VMEM((3 * SHARE, OUTER, 2 * INNER), F32),
            *[blocks] * 10,
            pltpu.VMEM((positions, channels), BF16),
            pltpu.VMEM((positions, channels), F32),
            pltpu.SemaphoreType.DMA((11,)),
            pltpu.SemaphoreType.DMA((2,)),
            pltpu.SemaphoreType.DMA((5,)),
            pltpu.SemaphoreType.DMA((5,)),
            pltpu.SemaphoreType.DMA((5,)),
        ],
        compiler_params=pltpu.CompilerParams(collective_id=0, has_side_effects=True, vmem_limit_bytes=48 << 20),
        name="two_strand_gradients",
    )(
        base_ids, embedding, gate_values.reshape(positions, channels), filter_kernel,
        complement.reshape(1, -1), output_gradient.reshape(positions, channels),
        *[jnp.asarray(table) for table in tables],
    )
    return gate_gradient[None], filter_gradient


def solution(mesh):
    in_specs = (
        P(None, "seq"),
        P(None, "chan"),
        P(None, "seq", "chan"),
        P("seq", "chan"),
        P(),
        P(None, "seq", "chan"),
    )
    out_specs = (P(None, "seq", "chan"), P("seq", "chan"))
    return jax.shard_map(shards, mesh=mesh, in_specs=in_specs, out_specs=out_specs, check_vma=False)
```

time: 339 us -> 66.9 us (0.20)
  waiting for transfers between devices: 107 us -> 0 us
  matrix products: 101 us -> 0 us
  Pallas kernels: 0 us -> 53.9 us
  local copies, waits for them, and re-layouts: 48.1 us -> 11.9 us
  blocking collectives: 34 us -> 0 us
  other arithmetic: 24 us -> 0 us
  between operations: 13.9 us -> 0.66 us
  starting transfers between devices: 7.32 us -> 0 us
    dot_general x41 -> x0, matrix products: 101 us -> none  [the longest x8 43.2 us: forward_spectra(): return jnp.einsum('zkn,nm->zkm', turned, inner_table, precision=HIGHEST)]
    all_gather x3 -> x0, waiting for transfers between devices: 72 us -> none  [the longest x1 24.3 us: shards(): lax.all_gather(filter_kernel, 'chan', axis=1, tiled=True)]
    pallas_call x0 -> x1, Pallas kernels: none -> 53.9 us  [shards(): pl.pallas_call(kernel, out_shape=[jax.ShapeDtypeStruct((positions, channe...]
    all_to_all x1 -> x0, waiting for transfers between devices: 34.6 us -> none  [shards(): lax.all_to_all(to_senders(stacked, seq_count), 'seq', split_axis=0, conca...]
    all_to_all x1 -> x0, blocking collectives: 34 us -> none  [shards(): lax.all_to_all(to_owners(outputs, seq_count, positions), 'seq', split_axi...]
    transpose x3 -> x0, local copies, waits for them, and re-layouts: 10.9 us -> none  [the longest x1 5.28 us: from_senders(): ordered = spread.transpose(1, 2, 0, 3)]
    gather x3 -> x0, local copies, waits for them, and re-layouts: 10.2 us -> none  [the longest x1 3.42 us: shards(): jnp.take(whole_grad, partner_index, axis=2)]
    sin x9 -> x0, other arithmetic: 9.31 us -> none  [the longest x8 8.28 us: build_tables(): jnp.sin(twist_angle)]
  transfers between devices with their start and end apart: 4 -> 0, of which waited for: 4 -> 0; matrix products, arithmetic and copies ran while one was open for 5% -> 0% of each run, Pallas kernels for 0% -> 0%
where the time goes in v1:
time: 66.9 us; the launch traced here: 66.4 us
  Pallas kernels  53.9 us (81%)
  local copies, waits for them, and re-layouts  11.9 us (18%)
    pallas_call x1, Pallas kernels, shards(): pl.pallas_call(kernel, out_shape=[jax.ShapeDtypeStruct((positions, channe...  53.9 us
    unnamed x24, local copies, waits for them, and re-layouts  11.9 us

profile of v1, /device:TPU:1, one launch (start us, length us, event | category | flops | bytes accessed | tf_op | source)
XLA Modules:
  0.0 66.4 jit_solution(9981831404587016740)
XLA Ops:
  0.6 0.0 copy-start.8
  0.6 0.7 %copy-done.8 = s32[1,1024]{1,0:T(1,128)S(1)} copy-done((s32[1,1024]{1,0:T(1,128)S(1)}, s32[1,1024]{1,0:T(1,128)}, u32[]{:S(2)}) %copy-start.8) | copy-done | bytes 4120
  1.3 0.0 copy-start
  1.3 1.0 %copy-done = bf16[1,1024,256]{2,1,0:T(8,128)(2,1)S(1)} copy-done((bf16[1,1024,256]{2,1,0:T(8,128)(2,1)S(1)}, bf16[1,1024,256]{2,1,0:T(8,128)(2,1)}, u32[]{:S(2)}) %copy-start) | copy-done | bytes 524312
  2.4 0.0 copy-start.1
  2.4 1.0 %copy-done.1 = bf16[1024,256]{1,0:T(8,128)(2,1)S(1)} copy-done((bf16[1024,256]{1,0:T(8,128)(2,1)S(1)}, bf16[1024,256]{1,0:T(8,128)(2,1)}, u32[]{:S(2)}) %copy-start.1) | copy-done | bytes 524312
  3.4 0.0 copy-start.2
  3.4 1.0 %copy-done.2 = bf16[1,1024,256]{2,1,0:T(8,128)(2,1)S(1)} copy-done((bf16[1,1024,256]{2,1,0:T(8,128)(2,1)S(1)}, bf16[1,1024,256]{2,1,0:T(8,128)(2,1)}, u32[]{:S(2)}) %copy-start.2) | copy-done | bytes 524312
  4.4 0.0 copy-start.3
  4.4 1.0 %copy-done.3 = bf16[2,256,512]{2,1,0:T(8,128)(2,1)S(1)} copy-done((bf16[2,256,512]{2,1,0:T(8,128)(2,1)S(1)}, bf16[2,256,512]{2,1,0:T(8,128)(2,1)}, u32[]{:S(2)}) %copy-start.3) | copy-done | bytes 524312
  5.5 0.0 copy-start.4
  5.5 1.0 %copy-done.4 = bf16[2,512,256]{2,1,0:T(8,128)(2,1)S(1)} copy-done((bf16[2,512,256]{2,1,0:T(8,128)(2,1)S(1)}, bf16[2,512,256]{2,1,0:T(8,128)(2,1)}, u32[]{:S(2)}) %copy-start.4) | copy-done | bytes 524312
  6.5 0.0 copy-start.5
  6.5 0.9 %copy-done.5 = f32[2,256,128]{2,1,0:T(8,128)S(1)} copy-done((f32[2,256,128]{2,1,0:T(8,128)S(1)}, f32[2,256,128]{2,1,0:T(8,128)}, u32[]{:S(2)}) %copy-start.5) | copy-done | bytes 262168
  7.5 0.0 copy-start.6
  7.5 0.9 %copy-done.6 = bf16[2,256,256]{2,1,0:T(8,128)(2,1)S(1)} copy-done((bf16[2,256,256]{2,1,0:T(8,128)(2,1)S(1)}, bf16[2,256,256]{2,1,0:T(8,128)(2,1)}, u32[]{:S(2)}) %copy-start.6) | copy-done | bytes 262168
  8.4 0.0 copy-start.7
  8.4 0.9 %copy-done.7 = bf16[2,256,256]{2,1,0:T(8,128)(2,1)S(1)} copy-done((bf16[2,256,256]{2,1,0:T(8,128)(2,1)S(1)}, bf16[2,256,256]{2,1,0:T(8,128)(2,1)}, u32[]{:S(2)}) %copy-start.7) | copy-done | bytes 262168
  9.4 0.0 copy-start.9
  9.4 0.7 %copy-done.9 = s32[1024]{0:T(1024)S(1)} copy-done((s32[1024]{0:T(1024)S(1)}, s32[1024]{0:T(1024)}, u32[]{:S(2)}) %copy-start.9) | copy-done | bytes 4120
  10.1 0.0 copy-start.10
  10.1 0.7 %copy-done.10 = bf16[4,256]{1,0:T(4,128)(2,1)S(1)} copy-done((bf16[4,256]{1,0:T(4,128)(2,1)S(1)}, bf16[4,256]{1,0:T(4,128)(2,1)}, u32[]{:S(2)}) %copy-start.10) | copy-done | bytes 2072
  10.8 53.9 %two_strand_gradients.1 = (bf16[1024,256]{1,0:T(8,128)(2,1)S(1)}, f32[1024,256]{1,0:T(8,128)S(1)}) custom-call(s32[1,1024]{1,0:T(1,128)S(1)} %copy-done.8, bf16[4,256]{1,0:T(4,128)(2,1)S(1)} %copy-done.10, bf16[1024,256]{1,0:T(8,128)(2,1)S(1)} %bitcast.5, bf16[1024,256]{1,0:T(8,128)(2,1)S(1)} %copy-done.1, s32[1,1024]{1,0:T(1,128)S(1)} %bitcast.7, ...), custom_call_target="tpu_custom_call" | custom-call | tf_op jit(solution)/shard_map/two_strand_gradients/pallas_call | solution.py:368
  64.6 0.8 %copy.15 = bf16[1,1024,256]{2,1,0:T(8,128)(2,1)} copy(bf16[1,1024,256]{2,1,0:T(8,128)(2,1)S(1)} %bitcast.4) | data formatting | bytes 1048576
  65.4 1.0 %copy.16 = f32[1024,256]{1,0:T(8,128)} copy(f32[1024,256]{1,0:T(8,128)S(1)} %get-tuple-element.9) | data formatting | bytes 2097152
Async XLA Ops:
  0.6 0.7 %copy-start.8 = (s32[1,1024]{1,0:T(1,128)S(1)}, s32[1,1024]{1,0:T(1,128)}, u32[]{:S(2)}) copy-start(s32[1,1024]{1,0:T(1,128)} %ids_hbm.1) | copy-start | bytes 12292
  1.3 1.0 %copy-start = (bf16[1,1024,256]{2,1,0:T(8,128)(2,1)S(1)}, bf16[1,1024,256]{2,1,0:T(8,128)(2,1)}, u32[]{:S(2)}) copy-start(bf16[1,1024,256]{2,1,0:T(8,128)(2,1)} %param.13) | copy-start | bytes 1572868
  2.4 1.0 %copy-start.1 = (bf16[1024,256]{1,0:T(8,128)(2,1)S(1)}, bf16[1024,256]{1,0:T(8,128)(2,1)}, u32[]{:S(2)}) copy-start(bf16[1024,256]{1,0:T(8,128)(2,1)} %filt_hbm.1) | copy-start | bytes 1572868
  3.4 1.0 %copy-start.2 = (bf16[1,1024,256]{2,1,0:T(8,128)(2,1)S(1)}, bf16[1,1024,256]{2,1,0:T(8,128)(2,1)}, u32[]{:S(2)}) copy-start(bf16[1,1024,256]{2,1,0:T(8,128)(2,1)} %param.16) | copy-start | bytes 1572868
  4.4 1.0 %copy-start.3 = (bf16[2,256,512]{2,1,0:T(8,128)(2,1)S(1)}, bf16[2,256,512]{2,1,0:T(8,128)(2,1)}, u32[]{:S(2)}) copy-start(bf16[2,256,512]{2,1,0:T(8,128)(2,1)} %constant.11.clone.outer_back_hbm) | copy-start | bytes 1572868
  5.5 1.0 %copy-start.4 = (bf16[2,512,256]{2,1,0:T(8,128)(2,1)S(1)}, bf16[2,512,256]{2,1,0:T(8,128)(2,1)}, u32[]{:S(2)}) copy-start(bf16[2,512,256]{2,1,0:T(8,128)(2,1)} %constant.10.clone.outer_hbm) | copy-start | bytes 1572868
  6.5 0.9 %copy-start.5 = (f32[2,256,128]{2,1,0:T(8,128)S(1)}, f32[2,256,128]{2,1,0:T(8,128)}, u32[]{:S(2)}) copy-start(f32[2,256,128]{2,1,0:T(8,128)} %constant.14.clone.twist_hbm) | copy-start | bytes 786436
  7.5 0.9 %copy-start.6 = (bf16[2,256,256]{2,1,0:T(8,128)(2,1)S(1)}, bf16[2,256,256]{2,1,0:T(8,128)(2,1)}, u32[]{:S(2)}) copy-start(bf16[2,256,256]{2,1,0:T(8,128)(2,1)} %constant.13.clone.inner_back_hbm) | copy-start | bytes 786436
  8.4 0.9 %copy-start.7 = (bf16[2,256,256]{2,1,0:T(8,128)(2,1)S(1)}, bf16[2,256,256]{2,1,0:T(8,128)(2,1)}, u32[]{:S(2)}) copy-start(bf16[2,256,256]{2,1,0:T(8,128)(2,1)} %constant.12.clone.inner_hbm) | copy-start | bytes 786436
  9.4 0.7 %copy-start.9 = (s32[1024]{0:T(1024)S(1)}, s32[1024]{0:T(1024)}, u32[]{:S(2)}) copy-start(s32[1024]{0:T(1024)} %param.15) | copy-start | bytes 12292
  10.1 0.7 %copy-start.10 = (bf16[4,256]{1,0:T(4,128)(2,1)S(1)}, bf16[4,256]{1,0:T(4,128)(2,1)}, u32[]{:S(2)}) copy-start(bf16[4,256]{1,0:T(4,128)(2,1)} %emb_hbm.1) | copy-start | bytes 6148

commit v2 on v1

--- a/solution.py
+++ b/solution.py
@@ -25,6 +25,7 @@
 HALF = 2 * ROWS
 CHANNELS = 256
 ALL_CHANNELS = SHARDS * CHANNELS
+UNROLL = 1
 
 
 def two_factors():
@@ -75,15 +76,42 @@
     return split(outer), split(outer.T * (2.0 / window)), split(inner), split(inner.T), twists
 
 
-def device_at(step, seq, chan):
-    sy, sz, sx = lax.div(seq, 8), lax.rem(lax.div(seq, 4), 2), lax.rem(seq, 4)
-    z = lax.div(chan, 2) * 2 + sz
-    core = lax.rem(chan, 2)
-    x2 = lax.rem(sx + lax.rem(step, 4), 4)
-    y2 = lax.rem(sy + lax.rem(lax.div(step, 4), 4), 4)
-    z2 = lax.rem(z + lax.rem(lax.div(step, 16), 4), 4)
-    core2 = lax.rem(core + lax.div(step, 64), 2)
-    return y2 * 8 + lax.rem(z2, 2) * 4 + x2, lax.div(z2, 2) * 2 + core2
+FAR_FIRST = (2, 1, 3, 0)
+
+
+class Neighbours:
+    def __init__(self, seq, chan):
+        self.sy, self.sz, self.sx = lax.div(seq, 8), lax.rem(lax.div(seq, 4), 2), lax.rem(seq, 4)
+        self.sz_high, self.core = lax.div(chan, 2), lax.rem(chan, 2)
+        self.x = [lax.rem(self.sx + step, 4) for step in range(4)]
+        self.y = [lax.rem(self.sy + step, 4) * 8 for step in range(4)]
+        self.z_low = [lax.rem(self.sz + step, 2) * 4 for step in range(2)]
+
+    def layer(self, step):
+        z = lax.rem(self.sz_high * 2 + self.sz + lax.rem(step, 4), 4)
+        core = lax.rem(self.core + lax.div(step, 4), 2)
+        return lax.rem(z, 2) * 4, lax.div(z, 2) * 2 + core
+
+    def each_other(self, visit):
+        def around(step, own):
+            low, chan = self.layer(step)
+            for dy in FAR_FIRST:
+                for dx in FAR_FIRST:
+                    if not (own and dx == 0 and dy == 0):
+                        visit(self.y[dy] + low + self.x[dx], chan)
+
+        def body(step, carry):
+            around(step, False)
+            return carry
+
+        lax.fori_loop(1, 8, body, 0)
+        around(0, True)
+
+    def each_in_shard(self, visit):
+        for low in (1, 0):
+            for dy in FAR_FIRST:
+                for dx in FAR_FIRST:
+                    visit(self.y[dy] + self.z_low[low] + self.x[dx], low == 0 and dx == 0 and dy == 0)
 
 
 def route(comp_ref, seq, chan, perm_ref):
@@ -108,7 +136,7 @@
     totals = jnp.dot(hot, jnp.ones((ALL_CHANNELS, CHANNELS), BF16), preferred_element_type=F32)
     rank = rank.astype(jnp.int32)
     totals = totals.astype(jnp.int32)
-    left = {edge: totals[edge[0] * SHARDS + edge[1]][None] for edge in {e for f in FACTORS for e in f[0]}}
+    left = {edge: totals[edge[0] * SHARDS + edge[1]][None] for edge in sorted({e for f in FACTORS for e in f[0]})}
     taken = {edge: jnp.zeros((1, CHANNELS), jnp.int32) for edge in left}
     begin = jnp.zeros((1, CHANNELS), jnp.int32)
     me = chan * SEQ_DEVICES + seq
@@ -116,7 +144,7 @@
     code = jnp.zeros((1, CHANNELS), jnp.int32)
     for chosen, ends, partner in FACTORS:
         count = None
-        for edge in set(chosen):
+        for edge in sorted(set(chosen)):
             possible = left[edge] if chosen.count(edge) == 1 else lax.shift_right_logical(left[edge], 1)
             count = possible if count is None else jnp.minimum(count, possible)
         for edge in sorted(set(chosen)):
@@ -146,11 +174,12 @@
     gate_out, filt_out,
     ids, emb, gate, filt, comp, grad,
     outer, outer_back, inner, inner_back, twist,
-    perm, strided, letters, embedded, spectra,
+    perm, strided, letters, embedded, spectra_k, spectra_g, spectra_u,
     send_k, send_g, send_u, recv_k, recv_g, recv_u,
     send_du, send_dk, recv_du, recv_dk, gate_vmem, filt_vmem,
     load_sem, store_sem, local_sem, send_sem, recv_sem,
 ):
+    spectra = (spectra_k, spectra_g, spectra_u)
     seq, chan = lax.axis_index("seq"), lax.axis_index("chan")
     me = chan * SEQ_DEVICES + seq
     loads = {}
@@ -165,11 +194,10 @@
 
     barrier = pltpu.get_barrier_semaphore()
 
-    def greet(step, carry):
-        pl.semaphore_signal(barrier, inc=1, device_id=device_at(step, seq, chan), device_id_type=MESH)
-        return carry
-
-    lax.fori_loop(1, DEVICES, greet, 0)
+    near = Neighbours(seq, chan)
+    near.each_other(
+        lambda seq2, chan2: pl.semaphore_signal(barrier, inc=1, device_id=(seq2, chan2), device_id_type=MESH)
+    )
 
     loads[0].wait()
     code = route(comp, seq, chan, perm)
@@ -188,15 +216,13 @@
     def post(source, target, index):
         pltpu.make_async_copy(source.at[me], target.at[me], local_sem.at[index]).start()
 
-        def one(step, carry):
-            seq2, chan2 = device_at(lax.rem(step * 37, DEVICES), seq, chan)
+        def one(seq2, chan2):
             pltpu.make_async_remote_copy(
                 source.at[chan2 * SEQ_DEVICES + seq2], target.at[me], send_sem.at[index], recv_sem.at[index],
                 device_id=(seq2, chan2), device_id_type=MESH,
             ).start()
-            return carry
-
-        lax.fori_loop(1, DEVICES, one, 0)
+
+        near.each_other(one)
 
     def arrived(source, target, index):
         pltpu.make_async_copy(source.at[me], target.at[me], local_sem.at[index]).wait()
@@ -270,51 +296,53 @@
         return jnp.concatenate(halves, axis=1).reshape(SEQ_DEVICES, HALF, LANES).astype(BF16)
 
     def spectrum(kind, channel):
-        both = spectra[kind * SHARE + channel]
+        both = spectra[kind][channel]
         return both[:, :INNER], both[:, INNER:]
 
     def partner_of(channel):
         return lax.rem(lax.shift_right_logical(code, 3 * channel), SHARE)
 
+    def forward_shard(received, kind, finish, shard):
+        both = forward(received, shard)
+        for slot in range(2):
+            channel = 2 * shard + slot
+            spectra[kind][channel] = finish(both[slot * OUTER : (slot + 1) * OUTER], channel)
+
     def all_forward(received, kind, finish):
         def body(shard, carry):
-            both = forward(received, shard)
-            for slot in range(2):
-                channel = 2 * shard + slot
-                spectra[kind * SHARE + channel] = finish(both[slot * OUTER : (slot + 1) * OUTER], channel)
+            forward_shard(received, kind, finish, shard)
             return carry
 
+        lax.fori_loop(0, SHARDS, body, 0, unroll=UNROLL)
+
+    def all_backward(prepare, combine, source, target, index):
+        def body(turn, carry):
+            shard = lax.rem(chan + 1 + turn, SHARDS)
+            base = shard * SEQ_DEVICES
+            prepare(shard)
+            source[pl.ds(base, SEQ_DEVICES)] = backward([combine(2 * shard + slot) for slot in range(2)])
+
+            def one(seq2, own):
+                def other():
+                    pltpu.make_async_remote_copy(
+                        source.at[base + seq2], target.at[me], send_sem.at[index], recv_sem.at[index],
+                        device_id=(seq2, shard), device_id_type=MESH,
+                    ).start()
+
+                if own:
+                    pl.when(turn < SHARDS - 1)(other)
+                else:
+                    other()
+
+            near.each_in_shard(one)
+            return carry
+
         lax.fori_loop(0, SHARDS, body, 0)
-
-    def all_backward(combine, source, target, index):
-        pltpu_local = pltpu.make_async_copy(source.at[me], target.at[me], local_sem.at[index])
-
-        def body(turn, carry):
-            shard = lax.rem(chan + turn, SHARDS)
-            base = shard * SEQ_DEVICES
-            source[pl.ds(base, SEQ_DEVICES)] = backward([combine(2 * shard + slot) for slot in range(2)])
-
-            @pl.when(turn == 0)
-            def _():
-                pltpu_local.start()
-
-            def one(step, inner_carry):
-                seq2 = lax.rem(seq + step, SEQ_DEVICES)
-                pltpu.make_async_remote_copy(
-                    source.at[base + seq2], target.at[me], send_sem.at[index], recv_sem.at[index],
-                    device_id=(seq2, shard), device_id_type=MESH,
-                ).start()
-                return inner_carry
-
-            lax.fori_loop(jnp.where(turn == 0, 1, 0), SEQ_DEVICES, one, 0)
-            return carry
-
-        lax.fori_loop(0, SHARDS, body, 0)
+        pltpu.make_async_copy(source.at[me], target.at[me], local_sem.at[index]).start()
 
     arrived(send_k, recv_k, 0)
     all_forward(recv_k, 0, lambda both, channel: both)
     arrived(send_g, recv_g, 1)
-    all_forward(recv_g, 1, lambda both, channel: both)
 
     def input_spectrum(channel):
         k_real, k_imag = spectrum(0, channel)
@@ -323,7 +351,9 @@
         real, imag = k_real + p_real, p_imag - k_imag
         return g_real * real - g_imag * imag, g_real * imag + g_imag * real
 
-    all_backward(input_spectrum, send_du, recv_du, 3)
+    all_backward(
+        lambda shard: forward_shard(recv_g, 1, lambda both, channel: both, shard), input_spectrum, send_du, recv_du, 3
+    )
 
     def product(both, channel):
         g_real, g_imag = spectrum(1, channel)
@@ -338,7 +368,7 @@
         p_real, p_imag = spectrum(2, partner_of(channel))
         return real + p_real, imag - p_imag
 
-    all_backward(filter_spectrum, send_dk, recv_dk, 4)
+    all_backward(lambda shard: None, filter_spectrum, send_dk, recv_dk, 4)
 
     def give_back(received, scale, target):
         strided[...] = received[...].astype(F32).reshape(DEVICES * HALF, LANES)
@@ -369,7 +399,7 @@
         kernel,
         out_shape=[
             jax.ShapeDtypeStruct((positions, channels), BF16),
-            jax.ShapeDtypeStruct((positions, channels), F32),
+            jax.ShapeDtypeStruct((positions, channels), BF16),
         ],
         in_specs=[pl.BlockSpec(memory_space=pl.ANY)] * 11,
         out_specs=[pl.BlockSpec(memory_space=pl.ANY)] * 2,
@@ -385,24 +415,24 @@
             pltpu.VMEM((DEVICES * HALF, LANES), F32),
             pltpu.VMEM((4, positions), BF16),
             pltpu.VMEM((ROWS, channels, LANES), F32),
-            pltpu.VMEM((3 * SHARE, OUTER, 2 * INNER), F32),
+            *[pltpu.VMEM((SHARE, OUTER, 2 * INNER), F32)] * 3,
             *[blocks] * 10,
             pltpu.VMEM((positions, channels), BF16),
-            pltpu.VMEM((positions, channels), F32),
+            pltpu.VMEM((positions, channels), BF16),
             pltpu.SemaphoreType.DMA((11,)),
             pltpu.SemaphoreType.DMA((2,)),
             pltpu.SemaphoreType.DMA((5,)),
             pltpu.SemaphoreType.DMA((5,)),
             pltpu.SemaphoreType.DMA((5,)),
         ],
-        compiler_params=pltpu.CompilerParams(collective_id=0, has_side_effects=True, vmem_limit_bytes=48 << 20),
+        compiler_params=pltpu.CompilerParams(collective_id=0, has_side_effects=True, vmem_limit_bytes=62 << 20),
         name="two_strand_gradients",
     )(
         base_ids, embedding, gate_values.reshape(positions, channels), filter_kernel,
         complement.reshape(1, -1), output_gradient.reshape(positions, channels),
         *[jnp.asarray(table) for table in tables],
     )
-    return gate_gradient[None], filter_gradient
+    return gate_gradient[None], filter_gradient.astype(F32)
 
 
 def solution(mesh):

time: 66.9 us -> 51.5 us (0.77)
  local copies, waits for them, and re-layouts: 11.9 us -> 0.8 us
  Pallas kernels: 53.9 us -> 47.7 us
  other arithmetic: 0 us -> 2.14 us
    unnamed x24 -> x3, local copies, waits for them, and re-layouts: 11.9 us -> 0.8 us
    pallas_call x1, Pallas kernels: 53.9 us -> 47.7 us  [shards(): pl.pallas_call(kernel, out_shape=[jax.ShapeDtypeStruct((positions, channe...]
    convert_element_type x0 -> x1, other arithmetic: none -> 2.14 us  [shards(): return (gate_gradient[None], filter_gradient.astype(F32))]
where the time goes in v2:
time: 51.5 us; the launch traced here: 51.3 us
  Pallas kernels  47.7 us (93%)
  other arithmetic  2.14 us (4%)
  local copies, waits for them, and re-layouts  0.8 us (2%)
  between operations  0.65 us (1%)
    pallas_call x1, Pallas kernels, shards(): pl.pallas_call(kernel, out_shape=[jax.ShapeDtypeStruct((positions, channe...  47.7 us
    convert_element_type x1, other arithmetic, shards(): return (gate_gradient[None], filter_gradient.astype(F32))  2.14 us

profile of v2, /device:TPU:1, one launch (start us, length us, event | category | flops | bytes accessed | tf_op | source)
XLA Modules:
  0.0 51.3 jit_solution(11412990067980184441)
XLA Ops:
  0.6 47.7 %two_strand_gradients.1 = (bf16[1024,256]{1,0:T(8,128)(2,1)}, bf16[1024,256]{1,0:T(8,128)(2,1)}) custom-call(s32[1,1024]{1,0:T(1,128)} %ids_hbm.1, bf16[4,256]{1,0:T(4,128)(2,1)} %emb_hbm.1, bf16[1024,256]{1,0:T(8,128)(2,1)} %bitcast.5, bf16[1024,256]{1,0:T(8,128)(2,1)} %filt_hbm.1, s32[1,1024]{1,0:T(1,128)} %bitcast.7, bf16[1024,256]{1,0:T(8,128)(2,1)} %bitcast.6, ...), custom_call_target="tpu_custom_call" | custom-call | tf_op jit(solution)/shard_map/two_strand_gradients/pallas_call | solution.py:398
  48.4 0.0 copy-start
  48.4 2.1 %convert_element_type.3 = f32[1024,256]{1,0:T(8,128)} convert(bf16[1024,256]{1,0:T(8,128)(2,1)} %get-tuple-element.5) | non-fusion elementwise | flops 262144 | bytes 1572864 | tf_op jit(solution)/shard_map/convert_element_type | solution.py:435
  50.5 0.0 copy-done
  50.5 0.8 %copy.14 = bf16[1,1024,256]{2,1,0:T(8,128)(2,1)} copy(bf16[1,1024,256]{2,1,0:T(8,128)(2,1)S(1)} %bitcast.4) | data formatting | bytes 1048576
Async XLA Ops:
  48.4 2.2 %copy-start = (bf16[1024,256]{1,0:T(8,128)(2,1)S(1)}, bf16[1024,256]{1,0:T(8,128)(2,1)}, u32[]{:S(2)}) copy-start(bf16[1024,256]{1,0:T(8,128)(2,1)} %get-tuple-element.4) | copy-start | bytes 1572868

commit v3 on v2

--- a/solution.py
+++ b/solution.py
@@ -25,7 +25,7 @@
 HALF = 2 * ROWS
 CHANNELS = 256
 ALL_CHANNELS = SHARDS * CHANNELS
-UNROLL = 1
+UNROLL = 4
 
 
 def two_factors():
@@ -337,7 +337,7 @@
             near.each_in_shard(one)
             return carry
 
-        lax.fori_loop(0, SHARDS, body, 0)
+        lax.fori_loop(0, SHARDS, body, 0, unroll=UNROLL)
         pltpu.make_async_copy(source.at[me], target.at[me], local_sem.at[index]).start()
 
     arrived(send_k, recv_k, 0)
@@ -351,9 +351,8 @@
         real, imag = k_real + p_real, p_imag - k_imag
         return g_real * real - g_imag * imag, g_real * imag + g_imag * real
 
-    all_backward(
-        lambda shard: forward_shard(recv_g, 1, lambda both, channel: both, shard), input_spectrum, send_du, recv_du, 3
-    )
+    all_forward(recv_g, 1, lambda both, channel: both)
+    all_backward(lambda shard: None, input_spectrum, send_du, recv_du, 3)
 
     def product(both, channel):
         g_real, g_imag = spectrum(1, channel)

time: 51.5 us -> 49.2 us (0.955)
  Pallas kernels: 47.7 us -> 45.5 us
    pallas_call x1, Pallas kernels: 47.7 us -> 45.5 us  [shards(): pl.pallas_call(kernel, out_shape=[jax.ShapeDtypeStruct((positions, channe...]
where the time goes in v3:
time: 49.2 us; the launch traced here: 49.1 us
  Pallas kernels  45.5 us (92%)
  other arithmetic  2.14 us (4%)
  local copies, waits for them, and re-layouts  0.8 us (2%)
  between operations  0.65 us (1%)
    pallas_call x1, Pallas kernels, shards(): pl.pallas_call(kernel, out_shape=[jax.ShapeDtypeStruct((positions, channe...  45.5 us
    convert_element_type x1, other arithmetic, shards(): return (gate_gradient[None], filter_gradient.astype(F32))  2.14 us

profile of v3, /device:TPU:1, one launch (start us, length us, event | category | flops | bytes accessed | tf_op | source)
XLA Modules:
  0.0 49.1 jit_solution(2646391155784623222)
XLA Ops:
  0.6 45.5 %two_strand_gradients.1 = (bf16[1024,256]{1,0:T(8,128)(2,1)}, bf16[1024,256]{1,0:T(8,128)(2,1)}) custom-call(s32[1,1024]{1,0:T(1,128)} %ids_hbm.1, bf16[4,256]{1,0:T(4,128)(2,1)} %emb_hbm.1, bf16[1024,256]{1,0:T(8,128)(2,1)} %bitcast.5, bf16[1024,256]{1,0:T(8,128)(2,1)} %filt_hbm.1, s32[1,1024]{1,0:T(1,128)} %bitcast.7, bf16[1024,256]{1,0:T(8,128)(2,1)} %bitcast.6, ...), custom_call_target="tpu_custom_call" | custom-call | tf_op jit(solution)/shard_map/two_strand_gradients/pallas_call | solution.py:397
  46.2 0.0 copy-start
  46.2 2.1 %convert_element_type.3 = f32[1024,256]{1,0:T(8,128)} convert(bf16[1024,256]{1,0:T(8,128)(2,1)} %get-tuple-element.5) | non-fusion elementwise | flops 262144 | bytes 1572864 | tf_op jit(solution)/shard_map/convert_element_type | solution.py:434
  48.3 0.0 copy-done
  48.3 0.8 %copy.14 = bf16[1,1024,256]{2,1,0:T(8,128)(2,1)} copy(bf16[1,1024,256]{2,1,0:T(8,128)(2,1)S(1)} %bitcast.4) | data formatting | bytes 1048576
Async XLA Ops:
  46.2 2.2 %copy-start = (bf16[1024,256]{1,0:T(8,128)(2,1)S(1)}, bf16[1024,256]{1,0:T(8,128)(2,1)}, u32[]{:S(2)}) copy-start(bf16[1024,256]{1,0:T(8,128)(2,1)} %get-tuple-element.4) | copy-start | bytes 1572868

commit v4 on v3

--- a/solution.py
+++ b/solution.py
@@ -85,7 +85,6 @@
         self.sz_high, self.core = lax.div(chan, 2), lax.rem(chan, 2)
         self.x = [lax.rem(self.sx + step, 4) for step in range(4)]
         self.y = [lax.rem(self.sy + step, 4) * 8 for step in range(4)]
-        self.z_low = [lax.rem(self.sz + step, 2) * 4 for step in range(2)]
 
     def layer(self, step):
         z = lax.rem(self.sz_high * 2 + self.sz + lax.rem(step, 4), 4)
@@ -106,12 +105,6 @@
 
         lax.fori_loop(1, 8, body, 0)
         around(0, True)
-
-    def each_in_shard(self, visit):
-        for low in (1, 0):
-            for dy in FAR_FIRST:
-                for dx in FAR_FIRST:
-                    visit(self.y[dy] + self.z_low[low] + self.x[dx], low == 0 and dx == 0 and dy == 0)
 
 
 def route(comp_ref, seq, chan, perm_ref):
@@ -168,15 +161,19 @@
     return jnp.max(code)
 
 
+def put_back(part, perm):
+    return lax.dot_general(part, perm[...], (((0,), (0,)), ((), ())), preferred_element_type=F32)
+
+
 def kernel(
     ids_hbm, emb_hbm, gate_hbm, filt_hbm, comp_hbm, grad_hbm,
     outer_hbm, outer_back_hbm, inner_hbm, inner_back_hbm, twist_hbm,
-    gate_out, filt_out,
+    gate_out, recv_dk, perm_out,
     ids, emb, gate, filt, comp, grad,
     outer, outer_back, inner, inner_back, twist,
     perm, strided, letters, embedded, spectra_k, spectra_g, spectra_u,
     send_k, send_g, send_u, recv_k, recv_g, recv_u,
-    send_du, send_dk, recv_du, recv_dk, gate_vmem, filt_vmem,
+    send_du, send_dk, recv_du, gate_vmem,
     load_sem, store_sem, local_sem, send_sem, recv_sem,
 ):
     spectra = (spectra_k, spectra_g, spectra_u)
@@ -201,6 +198,8 @@
 
     loads[0].wait()
     code = route(comp, seq, chan, perm)
+    perm_store = pltpu.make_async_copy(perm, perm_out, store_sem.at[1])
+    perm_store.start()
 
     def lay_out(source_of, target):
         for a in range(ROWS):
@@ -252,7 +251,6 @@
     loads[5].wait()
     turn_gate = turned(gate)
     lay_out(lambda a: turn_gate(a) * embedded[a], send_u)
-    post(send_u, recv_u, 2)
 
     for index in range(6, 11):
         loads[index].wait()
@@ -315,32 +313,15 @@
 
         lax.fori_loop(0, SHARDS, body, 0, unroll=UNROLL)
 
-    def all_backward(prepare, combine, source, target, index):
-        def body(turn, carry):
-            shard = lax.rem(chan + 1 + turn, SHARDS)
-            base = shard * SEQ_DEVICES
-            prepare(shard)
-            source[pl.ds(base, SEQ_DEVICES)] = backward([combine(2 * shard + slot) for slot in range(2)])
-
-            def one(seq2, own):
-                def other():
-                    pltpu.make_async_remote_copy(
-                        source.at[base + seq2], target.at[me], send_sem.at[index], recv_sem.at[index],
-                        device_id=(seq2, shard), device_id_type=MESH,
-                    ).start()
-
-                if own:
-                    pl.when(turn < SHARDS - 1)(other)
-                else:
-                    other()
-
-            near.each_in_shard(one)
+    def all_backward(combine, source):
+        def body(shard, carry):
+            source[pl.ds(shard * SEQ_DEVICES, SEQ_DEVICES)] = backward([combine(2 * shard + slot) for slot in range(2)])
             return carry
 
         lax.fori_loop(0, SHARDS, body, 0, unroll=UNROLL)
-        pltpu.make_async_copy(source.at[me], target.at[me], local_sem.at[index]).start()
 
     arrived(send_k, recv_k, 0)
+    post(send_u, recv_u, 2)
     all_forward(recv_k, 0, lambda both, channel: both)
     arrived(send_g, recv_g, 1)
 
@@ -352,7 +333,8 @@
         return g_real * real - g_imag * imag, g_real * imag + g_imag * real
 
     all_forward(recv_g, 1, lambda both, channel: both)
-    all_backward(lambda shard: None, input_spectrum, send_du, recv_du, 3)
+    all_backward(input_spectrum, send_du)
+    post(send_du, recv_du, 3)
 
     def product(both, channel):
         g_real, g_imag = spectrum(1, channel)
@@ -367,41 +349,61 @@
         p_real, p_imag = spectrum(2, partner_of(channel))
         return real + p_real, imag - p_imag
 
-    all_backward(lambda shard: None, filter_spectrum, send_dk, recv_dk, 4)
-
-    def give_back(received, scale, target):
-        strided[...] = received[...].astype(F32).reshape(DEVICES * HALF, LANES)
-        for a in range(ROWS):
-            part = scale(strided[pl.ds(a, CHANNELS, stride=ROWS), :], a).astype(BF16)
-            block = lax.dot_general(part, perm[...], (((0,), (0,)), ((), ())), preferred_element_type=F32)
-            target[pl.ds(a * LANES, LANES), :] = block.astype(target.dtype)
+    all_backward(filter_spectrum, send_dk)
+    post(send_dk, recv_dk, 4)
 
     arrived(send_du, recv_du, 3)
-    give_back(recv_du, lambda part, a: part * embedded[a], gate_vmem)
+    strided[...] = recv_du[...].astype(F32).reshape(DEVICES * HALF, LANES)
+    for a in range(ROWS):
+        part = (strided[pl.ds(a, CHANNELS, stride=ROWS), :] * embedded[a]).astype(BF16)
+        gate_vmem[pl.ds(a * LANES, LANES), :] = put_back(part, perm).astype(BF16)
     gate_store = pltpu.make_async_copy(gate_vmem, gate_out, store_sem.at[0])
     gate_store.start()
     arrived(send_dk, recv_dk, 4)
-    give_back(recv_dk, lambda part, a: part, filt_vmem)
-    filt_store = pltpu.make_async_copy(filt_vmem, filt_out, store_sem.at[1])
-    filt_store.start()
     for index, source in enumerate([send_k, send_g, send_u, send_du, send_dk]):
         left_here(source, index)
     gate_store.wait()
-    filt_store.wait()
+    perm_store.wait()
+
+
+def finish(gate_hbm, back_hbm, perm_hbm, gate_out, filt_out, gate, back, perm, strided, filt, load_sem, store_sem):
+    gate_load = pltpu.make_async_copy(gate_hbm, gate, load_sem.at[2])
+    gate_store = pltpu.make_async_copy(gate, gate_out, store_sem.at[ROWS])
+    back_load = pltpu.make_async_copy(back_hbm, back, load_sem.at[0])
+    perm_load = pltpu.make_async_copy(perm_hbm, perm, load_sem.at[1])
+    back_load.start()
+    perm_load.start()
+    gate_load.start()
+    back_load.wait()
+    strided[...] = back[...].astype(F32).reshape(DEVICES * HALF, LANES)
+    gate_load.wait()
+    gate_store.start()
+    perm_load.wait()
+    stores = []
+    for a in range(ROWS):
+        part = strided[pl.ds(a, CHANNELS, stride=ROWS), :].astype(BF16)
+        rows = pl.ds(a * LANES, LANES)
+        filt[rows, :] = put_back(part, perm)
+        stores.append(pltpu.make_async_copy(filt.at[rows], filt_out.at[rows], store_sem.at[a]))
+        stores[-1].start()
+    for store in stores:
+        store.wait()
+    gate_store.wait()
 
 
 def shards(base_ids, embedding, gate_values, filter_kernel, complement, output_gradient):
     positions, channels = filter_kernel.shape
     tables = transform_tables()
     blocks = pltpu.VMEM((DEVICES, HALF, LANES), BF16)
-    gate_gradient, filter_gradient = pl.pallas_call(
+    parts = pl.pallas_call(
         kernel,
         out_shape=[
             jax.ShapeDtypeStruct((positions, channels), BF16),
-            jax.ShapeDtypeStruct((positions, channels), BF16),
+            jax.ShapeDtypeStruct((DEVICES, HALF, LANES), BF16),
+            jax.ShapeDtypeStruct((channels, channels), BF16),
         ],
         in_specs=[pl.BlockSpec(memory_space=pl.ANY)] * 11,
-        out_specs=[pl.BlockSpec(memory_space=pl.ANY)] * 2,
+        out_specs=[pl.BlockSpec(memory_space=pl.ANY)] * 3,
         scratch_shapes=[
             pltpu.VMEM((1, positions), jnp.int32),
             pltpu.VMEM(embedding.shape, BF16),
@@ -415,8 +417,7 @@
             pltpu.VMEM((4, positions), BF16),
             pltpu.VMEM((ROWS, channels, LANES), F32),
             *[pltpu.VMEM((SHARE, OUTER, 2 * INNER), F32)] * 3,
-            *[blocks] * 10,
-            pltpu.VMEM((positions, channels), BF16),
+            *[blocks] * 9,
             pltpu.VMEM((positions, channels), BF16),
             pltpu.SemaphoreType.DMA((11,)),
             pltpu.SemaphoreType.DMA((2,)),
@@ -431,7 +432,27 @@
         complement.reshape(1, -1), output_gradient.reshape(positions, channels),
         *[jnp.asarray(table) for table in tables],
     )
-    return gate_gradient[None], filter_gradient.astype(F32)
+    gate_gradient, filter_gradient = pl.pallas_call(
+        finish,
+        out_shape=[
+            jax.ShapeDtypeStruct((positions, channels), BF16),
+            jax.ShapeDtypeStruct((positions, channels), F32),
+        ],
+        in_specs=[pl.BlockSpec(memory_space=pl.ANY)] * 3,
+        out_specs=[pl.BlockSpec(memory_space=pl.ANY)] * 2,
+        scratch_shapes=[
+            pltpu.VMEM((positions, channels), BF16),
+            blocks,
+            pltpu.VMEM((channels, channels), BF16),
+            pltpu.VMEM((DEVICES * HALF, LANES), F32),
+            pltpu.VMEM((positions, channels), F32),
+            pltpu.SemaphoreType.DMA((3,)),
+            pltpu.SemaphoreType.DMA((ROWS + 1,)),
+        ],
+        compiler_params=pltpu.CompilerParams(vmem_limit_bytes=62 << 20),
+        name="positions_by_channels",
+    )(*parts)
+    return gate_gradient[None], filter_gradient
 
 
 def solution(mesh):

time: 49.2 us -> 47.3 us (0.961)
  other arithmetic: 2.14 us -> 0 us
  Pallas kernels: 45.5 us -> 46.6 us
  local copies, waits for them, and re-layouts: 0.8 us -> 0 us
    pallas_call x0 -> x1, Pallas kernels: none -> 2.56 us  [shards(): pl.pallas_call(finish, out_shape=[jax.ShapeDtypeStruct((positions, channe...]
    convert_element_type x1 -> x0, other arithmetic: 2.14 us -> none  [shards(): return (gate_gradient[None], filter_gradient.astype(F32))]
    pallas_call x1, Pallas kernels: 45.5 us -> 44 us  [shards(): pl.pallas_call(kernel, out_shape=[jax.ShapeDtypeStruct((positions, channe...]
    unnamed x3 -> x0, local copies, waits for them, and re-layouts: 0.8 us -> none
where the time goes in v4:
time: 47.3 us; the launch traced here: 47.2 us
  Pallas kernels  46.6 us (99%)
  between operations  0.64 us (1%)
    pallas_call x1, Pallas kernels, shards(): pl.pallas_call(kernel, out_shape=[jax.ShapeDtypeStruct((positions, channe...  44 us
    pallas_call x1, Pallas kernels, shards(): pl.pallas_call(finish, out_shape=[jax.ShapeDtypeStruct((positions, channe...  2.56 us

profile of v4, /device:TPU:1, one launch (start us, length us, event | category | flops | bytes accessed | tf_op | source)
XLA Modules:
  0.0 47.2 jit_solution(17061537379569299706)
XLA Ops:
  0.6 44.0 %two_strand_gradients.1 = (bf16[1024,256]{1,0:T(8,128)(2,1)}, bf16[128,16,128]{2,1,0:T(8,128)(2,1)}, bf16[256,256]{1,0:T(8,128)(2,1)}) custom-call(s32[1,1024]{1,0:T(1,128)} %ids_hbm.1, bf16[4,256]{1,0:T(4,128)(2,1)} %emb_hbm.1, bf16[1024,256]{1,0:T(8,128)(2,1)} %bitcast.4, bf16[1024,256]{1,0:T(8,128)(2,1)} %filt_hbm.1, s32[1,1024]{1,0:T(1,128)} %bitcast.6, ...), custom_call_target="tpu_custom_call" | custom-call | tf_op jit(solution)/shard_map/two_strand_gradients/pallas_call | solution.py:398
  44.6 2.6 %positions_by_channels.1 = (bf16[1024,256]{1,0:T(8,128)(2,1)}, f32[1024,256]{1,0:T(8,128)}) custom-call(bf16[1024,256]{1,0:T(8,128)(2,1)} %get-tuple-element.7.gate_hbm, bf16[128,16,128]{2,1,0:T(8,128)(2,1)} %get-tuple-element.8.back_hbm, bf16[256,256]{1,0:T(8,128)(2,1)} %get-tuple-element.9.perm_hbm), custom_call_target="tpu_custom_call" | custom-call | tf_op jit(solution)/shard_map/positions_by_channels/pallas_call | solution.py:435

commit v5 on v4

--- a/solution.py
+++ b/solution.py
@@ -91,7 +91,7 @@
         core = lax.rem(self.core + lax.div(step, 4), 2)
         return lax.rem(z, 2) * 4, lax.div(z, 2) * 2 + core
 
-    def each_other(self, visit):
+    def each_in_half(self, other_core, visit):
         def around(step, own):
             low, chan = self.layer(step)
             for dy in FAR_FIRST:
@@ -103,8 +103,15 @@
             around(step, False)
             return carry
 
-        lax.fori_loop(1, 8, body, 0)
-        around(0, True)
+        if other_core:
+            lax.fori_loop(4, 8, body, 0)
+        else:
+            lax.fori_loop(1, 4, body, 0)
+            around(0, True)
+
+    def each_other(self, visit):
+        self.each_in_half(1, visit)
+        self.each_in_half(0, visit)
 
 
 def route(comp_ref, seq, chan, perm_ref):
@@ -212,16 +219,15 @@
             return lax.dot_general(perm[...], block, (((1,), (1,)), ((), ())), preferred_element_type=F32)
         return part
 
+    def send_block(source, target, index, seq2, chan2):
+        pltpu.make_async_remote_copy(
+            source.at[chan2 * SEQ_DEVICES + seq2], target.at[me], send_sem.at[index], recv_sem.at[index],
+            device_id=(seq2, chan2), device_id_type=MESH,
+        ).start()
+
     def post(source, target, index):
         pltpu.make_async_copy(source.at[me], target.at[me], local_sem.at[index]).start()
-
-        def one(seq2, chan2):
-            pltpu.make_async_remote_copy(
-                source.at[chan2 * SEQ_DEVICES + seq2], target.at[me], send_sem.at[index], recv_sem.at[index],
-                device_id=(seq2, chan2), device_id_type=MESH,
-            ).start()
-
-        near.each_other(one)
+        near.each_other(lambda seq2, chan2: send_block(source, target, index, seq2, chan2))
 
     def arrived(source, target, index):
         pltpu.make_async_copy(source.at[me], target.at[me], local_sem.at[index]).wait()
@@ -239,7 +245,6 @@
 
     loads[4].wait()
     lay_out(turned(grad), send_g)
-    post(send_g, recv_g, 1)
 
     loads[1].wait()
     loads[2].wait()
@@ -251,6 +256,8 @@
     loads[5].wait()
     turn_gate = turned(gate)
     lay_out(lambda a: turn_gate(a) * embedded[a], send_u)
+
+    post(send_g, recv_g, 1)
 
     for index in range(6, 11):
         loads[index].wait()
@@ -313,12 +320,18 @@
 
         lax.fori_loop(0, SHARDS, body, 0, unroll=UNROLL)
 
-    def all_backward(combine, source):
-        def body(shard, carry):
-            source[pl.ds(shard * SEQ_DEVICES, SEQ_DEVICES)] = backward([combine(2 * shard + slot) for slot in range(2)])
-            return carry
-
-        lax.fori_loop(0, SHARDS, body, 0, unroll=UNROLL)
+    def all_backward(combine, source, target, index):
+        for other_core in (1, 0):
+            core = lax.rem(near.core + other_core, 2)
+
+            def body(z_high, carry):
+                shard = 2 * z_high + core
+                source[pl.ds(shard * SEQ_DEVICES, SEQ_DEVICES)] = backward([combine(2 * shard + slot) for slot in range(2)])
+                return carry
+
+            lax.fori_loop(0, 2, body, 0, unroll=True)
+            near.each_in_half(other_core, lambda seq2, chan2: send_block(source, target, index, seq2, chan2))
+        pltpu.make_async_copy(source.at[me], target.at[me], local_sem.at[index]).start()
 
     arrived(send_k, recv_k, 0)
     post(send_u, recv_u, 2)
@@ -333,8 +346,7 @@
         return g_real * real - g_imag * imag, g_real * imag + g_imag * real
 
     all_forward(recv_g, 1, lambda both, channel: both)
-    all_backward(input_spectrum, send_du)
-    post(send_du, recv_du, 3)
+    all_backward(input_spectrum, send_du, recv_du, 3)
 
     def product(both, channel):
         g_real, g_imag = spectrum(1, channel)
@@ -349,8 +361,7 @@
         p_real, p_imag = spectrum(2, partner_of(channel))
         return real + p_real, imag - p_imag
 
-    all_backward(filter_spectrum, send_dk)
-    post(send_dk, recv_dk, 4)
+    all_backward(filter_spectrum, send_dk, recv_dk, 4)
 
     arrived(send_du, recv_du, 3)
     strided[...] = recv_du[...].astype(F32).reshape(DEVICES * HALF, LANES)

time: 47.3 us -> 45.3 us (0.958)
  Pallas kernels: 46.6 us -> 44.5 us
    pallas_call x1, Pallas kernels: 44 us -> 42 us  [shards(): pl.pallas_call(kernel, out_shape=[jax.ShapeDtypeStruct((positions, channe...]
where the time goes in v5:
time: 45.3 us; the launch traced here: 45.2 us
  Pallas kernels  44.5 us (98%)
  between operations  0.64 us (1%)
    pallas_call x1, Pallas kernels, shards(): pl.pallas_call(kernel, out_shape=[jax.ShapeDtypeStruct((positions, channe...  42 us
    pallas_call x1, Pallas kernels, shards(): pl.pallas_call(finish, out_shape=[jax.ShapeDtypeStruct((positions, channe...  2.56 us

profile of v5, /device:TPU:1, one launch (start us, length us, event | category | flops | bytes accessed | tf_op | source)
XLA Modules:
  0.0 45.2 jit_solution(6046406499870950692)
XLA Ops:
  0.6 42.0 %two_strand_gradients.1 = (bf16[1024,256]{1,0:T(8,128)(2,1)}, bf16[128,16,128]{2,1,0:T(8,128)(2,1)}, bf16[256,256]{1,0:T(8,128)(2,1)}) custom-call(s32[1,1024]{1,0:T(1,128)} %ids_hbm.1, bf16[4,256]{1,0:T(4,128)(2,1)} %emb_hbm.1, bf16[1024,256]{1,0:T(8,128)(2,1)} %bitcast.4, bf16[1024,256]{1,0:T(8,128)(2,1)} %filt_hbm.1, s32[1,1024]{1,0:T(1,128)} %bitcast.6, ...), custom_call_target="tpu_custom_call" | custom-call | tf_op jit(solution)/shard_map/two_strand_gradients/pallas_call | solution.py:409
  42.6 2.6 %positions_by_channels.1 = (bf16[1024,256]{1,0:T(8,128)(2,1)}, f32[1024,256]{1,0:T(8,128)}) custom-call(bf16[1024,256]{1,0:T(8,128)(2,1)} %get-tuple-element.7.gate_hbm, bf16[128,16,128]{2,1,0:T(8,128)(2,1)} %get-tuple-element.8.back_hbm, bf16[256,256]{1,0:T(8,128)(2,1)} %get-tuple-element.9.perm_hbm), custom_call_target="tpu_custom_call" | custom-call | tf_op jit(solution)/shard_map/positions_by_channels/pallas_call | solution.py:446

commit v6 on v5

--- a/solution.py
+++ b/solution.py
@@ -194,6 +194,7 @@
     ]
     for index, (source, target) in enumerate(sources):
         loads[index] = pltpu.make_async_copy(source, target, load_sem.at[index])
+    for index in (0, 3):
         loads[index].start()
 
     barrier = pltpu.get_barrier_semaphore()
@@ -202,6 +203,9 @@
     near.each_other(
         lambda seq2, chan2: pl.semaphore_signal(barrier, inc=1, device_id=(seq2, chan2), device_id_type=MESH)
     )
+
+    for index in (4, 1, 2, 5, 6, 7, 8, 9, 10):
+        loads[index].start()
 
     loads[0].wait()
     code = route(comp, seq, chan, perm)

time: 45.3 us -> 45.3 us (level)
  no operation moved by 1% of the time
where the time goes in v6:
time: 45.3 us; the launch traced here: 45.2 us
  Pallas kernels  44.5 us (98%)
  between operations  0.64 us (1%)
    pallas_call x1, Pallas kernels, shards(): pl.pallas_call(kernel, out_shape=[jax.ShapeDtypeStruct((positions, channe...  42 us
    pallas_call x1, Pallas kernels, shards(): pl.pallas_call(finish, out_shape=[jax.ShapeDtypeStruct((positions, channe...  2.56 us

profile of v6, /device:TPU:1, one launch (start us, length us, event | category | flops | bytes accessed | tf_op | source)
XLA Modules:
  0.0 45.2 jit_solution(12504199847698566050)
XLA Ops:
  0.6 42.0 %two_strand_gradients.1 = (bf16[1024,256]{1,0:T(8,128)(2,1)}, bf16[128,16,128]{2,1,0:T(8,128)(2,1)}, bf16[256,256]{1,0:T(8,128)(2,1)}) custom-call(s32[1,1024]{1,0:T(1,128)} %ids_hbm.1, bf16[4,256]{1,0:T(4,128)(2,1)} %emb_hbm.1, bf16[1024,256]{1,0:T(8,128)(2,1)} %bitcast.4, bf16[1024,256]{1,0:T(8,128)(2,1)} %filt_hbm.1, s32[1,1024]{1,0:T(1,128)} %bitcast.6, ...), custom_call_target="tpu_custom_call" | custom-call | tf_op jit(solution)/shard_map/two_strand_gradients/pallas_call | solution.py:413
  42.6 2.6 %positions_by_channels.1 = (bf16[1024,256]{1,0:T(8,128)(2,1)}, f32[1024,256]{1,0:T(8,128)}) custom-call(bf16[1024,256]{1,0:T(8,128)(2,1)} %get-tuple-element.7.gate_hbm, bf16[128,16,128]{2,1,0:T(8,128)(2,1)} %get-tuple-element.8.back_hbm, bf16[256,256]{1,0:T(8,128)(2,1)} %get-tuple-element.9.perm_hbm), custom_call_target="tpu_custom_call" | custom-call | tf_op jit(solution)/shard_map/positions_by_channels/pallas_call | solution.py:450
